TPU v7x, 256 devices: a whole 4x4x8 slice. The times are simulated.
256 devices in a mesh: ctx: 8 (over x, y_hi), fsdp: 32 (over z, y_lo, core).
Axes of the slice: x: 4, y: 4 (y_hi: 2, y_lo: 2; y = y_hi * 2 + y_lo), z: 8, core: 2. Of those that a mesh axis runs over, the one named last changes fastest.
Arguments:
- queries: bfloat16 [768, 4, 8192], P('fsdp'), may hold values from -14 to 14
- key_pages: bfloat16 [192, 64, 1024], P('ctx'), may hold values from -7 to 7
- value_pages: bfloat16 [192, 64, 1024], P('ctx'), may hold values from -6 to 6
- new_keys: bfloat16 [768, 4, 8, 128], P('fsdp', None, 'ctx'), may hold values from -7 to 7
- new_values: bfloat16 [768, 4, 8, 128], P('fsdp', None, 'ctx'), may hold values from -6 to 6
- page_table: int32 [768, 16], P('fsdp'), may hold values from 0 to 191, as said below
- lengths: int32 [768], P('fsdp'), may hold values from 1 to 1024
- parents: int32 [768, 4], P('fsdp'), may hold values from -1 to 2, as said below
- o_weight: bfloat16 [8192, 8192], P('ctx', 'fsdp'), may hold values from -0.0625 to 0.0625
Outputs:
- mixed: bfloat16 [768, 4, 8192], P('fsdp', None, 'ctx')
Inputs may be any that keep to these rules, and one draw needn't show every extreme that they name: `page_table`: each row holds 16 distinct page ids; aligned groups of 8 consecutive trajectories share their first 8 entries, which lie below 96; the other entries are drawn for each trajectory from the common pool of pages at or above 96, so many trajectories reuse them. parents[t, i] lies below i; parents[t, 0] is -1.
All inputs are finite; a program needn't handle non-finite values.
Results may differ from a plain program's by a relative error of at most 0.0053.
Values may be sent and summed in bfloat16 or wider, within the bound.
A program may use at most 128 MiB of HBM per device.

v0:
```python
import jax
import jax.numpy as jnp
from jax import lax
from jax.sharding import PartitionSpec as P


def ancestry(parents, count):
    index = jnp.arange(count, dtype=jnp.int32)
    reach = parents[:, :, None] * 0 + index[None, None, :] == index[None, :, None]
    current = parents
    for level in range(count):
        reach = reach | (current[:, :, None] == index[None, None, :])
        hitting = (current[:, :, None] == index[None, None, :]).astype(jnp.int32)
        upward = jnp.sum(hitting * parents[:, None, :], axis=-1)
        current = jnp.where(current >= 0, upward, -1)
    return reach


def live_table(page_table, lengths, page_ids, page_len):
    table_len = page_table.shape[1]
    matching = (page_table[:, :, None] == page_ids[None, None, :]).astype(jnp.int32)
    slot_number = (
        jnp.sum(matching * (jnp.arange(table_len, dtype=jnp.int32) + 1)[None, :, None], axis=1) - 1
    )
    offsets = jnp.arange(page_len, dtype=jnp.int32)
    return (slot_number[:, :, None] >= 0) & (
        slot_number[:, :, None] * page_len + offsets[None, None, :] < lengths[:, None, None]
    )


def page_attention(query_heads, key_pages, value_pages, live_all, stride, scale):
    rows, kv_count, group, head_size = query_heads.shape
    traj = live_all.shape[0]
    new = rows // traj
    page_count, page_len, _ = key_pages.shape

    def page_step(turn, carry):
        run_max, run_sum, run_out = carry
        keys_step = lax.dynamic_slice_in_dim(key_pages, stride * turn, stride, 0).reshape(
            stride, page_len, kv_count, head_size
        )
        values_step = lax.dynamic_slice_in_dim(value_pages, stride * turn, stride, 0).reshape(
            stride, page_len, kv_count, head_size
        )
        live_step = lax.dynamic_slice_in_dim(live_all, stride * turn, stride, 1)
        live_rows = jnp.broadcast_to(live_step[:, None], (traj, new, stride, page_len)).reshape(
            rows, 1, 1, stride, page_len
        )
        scores = (
            jnp.einsum(
                "rkgd,pokd->rkgpo", query_heads, keys_step, preferred_element_type=jnp.float32
            )
            * scale
        )
        block_max = jnp.max(jnp.where(live_rows, scores, -1e30), axis=-1)
        expo = jnp.where(live_rows, jnp.exp(scores - block_max[..., None]), 0.0)
        block_sum = jnp.sum(expo, axis=-1)
        weights = expo.astype(jnp.bfloat16)
        block_out = jnp.einsum(
            "rkgpo,pokd->rkgpd", weights, values_step, preferred_element_type=jnp.float32
        )
        next_max = jnp.maximum(run_max, jnp.max(block_max, axis=-1))
        keep = jnp.exp(run_max - next_max)
        factor = jnp.exp(block_max - next_max[..., None])
        next_sum = run_sum * keep + jnp.sum(block_sum * factor, axis=-1)
        next_out = run_out * keep[..., None] + jnp.sum(block_out * factor[..., None], axis=-2)
        return (next_max, next_sum, next_out)

    start_max = jnp.full((rows, kv_count, group), -1e30, jnp.float32)
    start_sum = jnp.zeros((rows, kv_count, group), jnp.float32)
    start_out = jnp.zeros((rows, kv_count, group, head_size), jnp.float32)
    return lax.fori_loop(0, page_count // stride, page_step, (start_max, start_sum, start_out))


def shards(
    queries, key_pages, value_pages, new_keys, new_values, page_table, lengths, parents, o_weight
):
    ctx_count = lax.axis_size("ctx")
    ctx_index = lax.axis_index("ctx")
    traj, new, _ = queries.shape
    kv_local = new_keys.shape[2]
    head_size = new_keys.shape[3]
    kv_total = kv_local * ctx_count
    heads = queries.shape[2] // head_size
    group = heads // kv_total
    rows = traj * new
    pages_local, page_len, _ = key_pages.shape
    scale = 1.0 / head_size**0.5
    query_heads = queries.reshape(rows, kv_total, group, head_size)
    own_heads = lax.dynamic_slice_in_dim(query_heads, ctx_index * kv_local, kv_local, 1)
    page_ids = ctx_index * pages_local + jnp.arange(pages_local, dtype=jnp.int32)
    live_all = live_table(page_table, lengths, page_ids, page_len)
    local_max, local_sum, local_out = page_attention(
        query_heads, key_pages, value_pages, live_all, 2, scale
    )
    all_out, all_max, all_sum = (
        lax.all_to_all(local_out[None], "ctx", split_axis=2, concat_axis=0, tiled=True),
        lax.all_to_all(local_max[None], "ctx", split_axis=2, concat_axis=0, tiled=True),
        lax.all_to_all(local_sum[None], "ctx", split_axis=2, concat_axis=0, tiled=True),
    )
    ctx_max = jnp.max(all_max, axis=0)
    weighing = jnp.exp(all_max - ctx_max[None])
    ctx_out = jnp.sum(all_out * weighing[..., None], axis=0)
    ctx_sum = jnp.sum(all_sum * weighing, axis=0)
    own_queries = own_heads.reshape(traj, new, kv_local, group, head_size)
    new_scores = (
        jnp.einsum("tnkgd,tmkd->tnkgm", own_queries, new_keys, preferred_element_type=jnp.float32)
        * scale
    )
    seen = ancestry(parents, new)[:, :, None, None, :]
    new_max = jnp.max(jnp.where(seen, new_scores, -1e30), axis=-1)
    new_expo = jnp.where(seen, jnp.exp(new_scores - new_max[..., None]), 0.0)
    new_sum = jnp.sum(new_expo, axis=-1).reshape(rows, kv_local, group)
    new_weights = new_expo.astype(jnp.bfloat16)
    new_out = jnp.einsum(
        "tnkgm,tmkd->tnkgd", new_weights, new_values, preferred_element_type=jnp.float32
    )
    new_out = new_out.reshape(rows, kv_local, group, head_size)
    new_max = new_max.reshape(rows, kv_local, group)
    overall = jnp.maximum(ctx_max, new_max)
    ctx_factor = jnp.exp(ctx_max - overall)
    new_factor = jnp.exp(new_max - overall)
    numer = ctx_out * ctx_factor[..., None] + new_out * new_factor[..., None]
    denom = ctx_sum * ctx_factor + new_sum * new_factor
    attended = (
        (numer / denom[..., None]).reshape(rows, kv_local * group * head_size).astype(jnp.bfloat16)
    )
    partial_sum = jnp.dot(
        attended,
        lax.all_gather(o_weight, "fsdp", axis=1, tiled=True),
        preferred_element_type=jnp.float32,
    )
    mixed = lax.psum_scatter(partial_sum, "ctx", scatter_dimension=1, tiled=True).astype(
        jnp.bfloat16
    )
    return mixed.reshape(traj, new, mixed.shape[1])


def solution(mesh):
    placed = (
        P("fsdp", None, None),
        P("ctx", None, None),
        P("ctx", None, None),
        P("fsdp", None, "ctx", None),
        P("fsdp", None, "ctx", None),
        P("fsdp", None),
        P("fsdp"),
        P("fsdp", None),
        P("ctx", "fsdp"),
    )
    return jax.shard_map(
        shards, mesh=mesh, in_specs=placed, out_specs=P("fsdp", None, "ctx"), check_vma=False
    )
```

profile of v0, /device:TPU:12, one launch (start us, length us, event | category | flops | bytes accessed | tf_op | source)
XLA Modules:
  0.0 411.0 jit_solution(2929812573686913931)
XLA Ops:
  8.3 4.2 %reshape.258 = bf16[96,8,8,128]{3,2,1,0:T(8,128)(2,1)} reshape(bf16[24,4,8192]{2,1,0:T(4,128)(2,1)} %param.11) | data formatting | bytes 3145728 | tf_op jit(solution)/shard_map/reshape | solution.py:89
  12.6 3.6 copy.77
  17.1 219.7 %while.18 = (s32[]{:T(128)}, f32[96,8,8]{0,2,1:T(8,128)S(1)}, f32[96,8,8]{0,2,1:T(8,128)}, f32[96,8,8,128]{3,0,2,1:T(8,128)S(1)}, pred[24,24,64]{2,0,1:T(8,128)(...) while((s32[]{:T(128)}, f32[96,8,8]{0,2,1:T(8,128)S(1)}, ...), condition=%wide.region_7.8_spmd.clone, body=%wide.region_1.7_spmd.clone.sunk | while | flops 417638400 | bytes 41936164 | solution.py:72
  17.1 1.8 constant_dynamic-slice_fusion.7
  19.8 2.8 fusion.61
  22.7 1.9 copy-done.1
  24.6 2.7 fusion.62
  29.0 4.9 %fusion.64 = f32[96,8,8,128]{3,0,2,1:T(8,128)S(1)} fusion(f32[96,8,8,2]{0,2,3,1:T(8,128)S(1)} %get-tuple-element.305, f32[8,2,64,96,8]{3,2,4,1,0:T(8,128)} %copy-done.1, f32[96,8,8,2]{0,2,3,1:T(8,128)S(1)} %get-tuple-element.300, pred[96,2,64]{0,2,1:T(8,128)(4,1)S(1)} %copy.135, bf16[2,64,8,128,1]{3,2,1,0,4:T(8,128)(2,1)S(1)} %bitcast_bitcast_fusion.5), kind=kOutput, calls=%fused_computation.1.clone.1 | convolution fusion | flops 206831616 | bytes 6664192 | tf_op jit(solution)/shard_map/while/body/eval_jaxpr/rkgpo,pokd->rkgpd/dot_general | solution.py:59
  38.1 2.8 fusion.61
  40.9 1.9 copy-done.1
  42.8 2.7 fusion.62
  47.3 5.0 %fusion.64 = f32[96,8,8,128]{3,0,2,1:T(8,128)S(1)} fusion(f32[96,8,8,2]{0,2,3,1:T(8,128)S(1)} %get-tuple-element.305, f32[8,2,64,96,8]{3,2,4,1,0:T(8,128)} %copy-done.1, f32[96,8,8,2]{0,2,3,1:T(8,128)S(1)} %get-tuple-element.300, pred[96,2,64]{0,2,1:T(8,128)(4,1)S(1)} %copy.135, bf16[2,64,8,128,1]{3,2,1,0,4:T(8,128)(2,1)S(1)} %bitcast_bitcast_fusion.5), kind=kOutput, calls=%fused_computation.1.clone.1 | convolution fusion | flops 206831616 | bytes 6664192 | tf_op jit(solution)/shard_map/while/body/eval_jaxpr/rkgpo,pokd->rkgpd/dot_general | solution.py:59
  56.4 3.0 fusion.61
  59.4 1.9 copy-done.1
  61.3 2.7 fusion.62
  65.8 4.9 %fusion.64 = f32[96,8,8,128]{3,0,2,1:T(8,128)S(1)} fusion(f32[96,8,8,2]{0,2,3,1:T(8,128)S(1)} %get-tuple-element.305, f32[8,2,64,96,8]{3,2,4,1,0:T(8,128)} %copy-done.1, f32[96,8,8,2]{0,2,3,1:T(8,128)S(1)} %get-tuple-element.300, pred[96,2,64]{0,2,1:T(8,128)(4,1)S(1)} %copy.135, bf16[2,64,8,128,1]{3,2,1,0,4:T(8,128)(2,1)S(1)} %bitcast_bitcast_fusion.5), kind=kOutput, calls=%fused_computation.1.clone.1 | convolution fusion | flops 206831616 | bytes 6664192 | tf_op jit(solution)/shard_map/while/body/eval_jaxpr/rkgpo,pokd->rkgpd/dot_general | solution.py:59
  74.8 2.9 fusion.61
  77.7 1.9 copy-done.1
  79.6 2.7 fusion.62
  84.1 4.9 %fusion.64 = f32[96,8,8,128]{3,0,2,1:T(8,128)S(1)} fusion(f32[96,8,8,2]{0,2,3,1:T(8,128)S(1)} %get-tuple-element.305, f32[8,2,64,96,8]{3,2,4,1,0:T(8,128)} %copy-done.1, f32[96,8,8,2]{0,2,3,1:T(8,128)S(1)} %get-tuple-element.300, pred[96,2,64]{0,2,1:T(8,128)(4,1)S(1)} %copy.135, bf16[2,64,8,128,1]{3,2,1,0,4:T(8,128)(2,1)S(1)} %bitcast_bitcast_fusion.5), kind=kOutput, calls=%fused_computation.1.clone.1 | convolution fusion | flops 206831616 | bytes 6664192 | tf_op jit(solution)/shard_map/while/body/eval_jaxpr/rkgpo,pokd->rkgpd/dot_general | solution.py:59
  90.5 1.8 constant_dynamic-slice_fusion.7
  93.2 2.8 fusion.61
  96.1 1.9 copy-done.1
  98.0 2.7 fusion.62
  102.4 4.9 %fusion.64 = f32[96,8,8,128]{3,0,2,1:T(8,128)S(1)} fusion(f32[96,8,8,2]{0,2,3,1:T(8,128)S(1)} %get-tuple-element.305, f32[8,2,64,96,8]{3,2,4,1,0:T(8,128)} %copy-done.1, f32[96,8,8,2]{0,2,3,1:T(8,128)S(1)} %get-tuple-element.300, pred[96,2,64]{0,2,1:T(8,128)(4,1)S(1)} %copy.135, bf16[2,64,8,128,1]{3,2,1,0,4:T(8,128)(2,1)S(1)} %bitcast_bitcast_fusion.5), kind=kOutput, calls=%fused_computation.1.clone.1 | convolution fusion | flops 206831616 | bytes 6664192 | tf_op jit(solution)/shard_map/while/body/eval_jaxpr/rkgpo,pokd->rkgpd/dot_general | solution.py:59
  108.8 1.8 constant_dynamic-slice_fusion.7
  111.5 2.8 fusion.61
  114.3 1.9 copy-done.1
  116.2 2.7 fusion.62
  120.7 5.0 %fusion.64 = f32[96,8,8,128]{3,0,2,1:T(8,128)S(1)} fusion(f32[96,8,8,2]{0,2,3,1:T(8,128)S(1)} %get-tuple-element.305, f32[8,2,64,96,8]{3,2,4,1,0:T(8,128)} %copy-done.1, f32[96,8,8,2]{0,2,3,1:T(8,128)S(1)} %get-tuple-element.300, pred[96,2,64]{0,2,1:T(8,128)(4,1)S(1)} %copy.135, bf16[2,64,8,128,1]{3,2,1,0,4:T(8,128)(2,1)S(1)} %bitcast_bitcast_fusion.5), kind=kOutput, calls=%fused_computation.1.clone.1 | convolution fusion | flops 206831616 | bytes 6664192 | tf_op jit(solution)/shard_map/while/body/eval_jaxpr/rkgpo,pokd->rkgpd/dot_general | solution.py:59
  127.2 1.8 constant_dynamic-slice_fusion.7
  129.9 2.8 fusion.61
  132.7 1.9 copy-done.1
  134.6 2.7 fusion.62
  139.1 4.9 %fusion.64 = f32[96,8,8,128]{3,0,2,1:T(8,128)S(1)} fusion(f32[96,8,8,2]{0,2,3,1:T(8,128)S(1)} %get-tuple-element.305, f32[8,2,64,96,8]{3,2,4,1,0:T(8,128)} %copy-done.1, f32[96,8,8,2]{0,2,3,1:T(8,128)S(1)} %get-tuple-element.300, pred[96,2,64]{0,2,1:T(8,128)(4,1)S(1)} %copy.135, bf16[2,64,8,128,1]{3,2,1,0,4:T(8,128)(2,1)S(1)} %bitcast_bitcast_fusion.5), kind=kOutput, calls=%fused_computation.1.clone.1 | convolution fusion | flops 206831616 | bytes 6664192 | tf_op jit(solution)/shard_map/while/body/eval_jaxpr/rkgpo,pokd->rkgpd/dot_general | solution.py:59
  148.2 2.8 fusion.61
  151.0 1.9 copy-done.1
  152.9 2.7 fusion.62
  157.3 4.9 %fusion.64 = f32[96,8,8,128]{3,0,2,1:T(8,128)S(1)} fusion(f32[96,8,8,2]{0,2,3,1:T(8,128)S(1)} %get-tuple-element.305, f32[8,2,64,96,8]{3,2,4,1,0:T(8,128)} %copy-done.1, f32[96,8,8,2]{0,2,3,1:T(8,128)S(1)} %get-tuple-element.300, pred[96,2,64]{0,2,1:T(8,128)(4,1)S(1)} %copy.135, bf16[2,64,8,128,1]{3,2,1,0,4:T(8,128)(2,1)S(1)} %bitcast_bitcast_fusion.5), kind=kOutput, calls=%fused_computation.1.clone.1 | convolution fusion | flops 206831616 | bytes 6664192 | tf_op jit(solution)/shard_map/while/body/eval_jaxpr/rkgpo,pokd->rkgpd/dot_general | solution.py:59
  166.4 2.8 fusion.61
  169.3 1.9 copy-done.1
  171.2 2.7 fusion.62
  175.6 4.9 %fusion.64 = f32[96,8,8,128]{3,0,2,1:T(8,128)S(1)} fusion(f32[96,8,8,2]{0,2,3,1:T(8,128)S(1)} %get-tuple-element.305, f32[8,2,64,96,8]{3,2,4,1,0:T(8,128)} %copy-done.1, f32[96,8,8,2]{0,2,3,1:T(8,128)S(1)} %get-tuple-element.300, pred[96,2,64]{0,2,1:T(8,128)(4,1)S(1)} %copy.135, bf16[2,64,8,128,1]{3,2,1,0,4:T(8,128)(2,1)S(1)} %bitcast_bitcast_fusion.5), kind=kOutput, calls=%fused_computation.1.clone.1 | convolution fusion | flops 206831616 | bytes 6664192 | tf_op jit(solution)/shard_map/while/body/eval_jaxpr/rkgpo,pokd->rkgpd/dot_general | solution.py:59
  184.7 2.8 fusion.61
  187.5 1.9 copy-done.1
  189.4 2.7 fusion.62
  193.9 4.9 %fusion.64 = f32[96,8,8,128]{3,0,2,1:T(8,128)S(1)} fusion(f32[96,8,8,2]{0,2,3,1:T(8,128)S(1)} %get-tuple-element.305, f32[8,2,64,96,8]{3,2,4,1,0:T(8,128)} %copy-done.1, f32[96,8,8,2]{0,2,3,1:T(8,128)S(1)} %get-tuple-element.300, pred[96,2,64]{0,2,1:T(8,128)(4,1)S(1)} %copy.135, bf16[2,64,8,128,1]{3,2,1,0,4:T(8,128)(2,1)S(1)} %bitcast_bitcast_fusion.5), kind=kOutput, calls=%fused_computation.1.clone.1 | convolution fusion | flops 206831616 | bytes 6664192 | tf_op jit(solution)/shard_map/while/body/eval_jaxpr/rkgpo,pokd->rkgpd/dot_general | solution.py:59
  203.0 2.8 fusion.61
  205.8 1.9 copy-done.1
  207.7 2.7 fusion.62
  212.1 4.9 %fusion.64 = f32[96,8,8,128]{3,0,2,1:T(8,128)S(1)} fusion(f32[96,8,8,2]{0,2,3,1:T(8,128)S(1)} %get-tuple-element.305, f32[8,2,64,96,8]{3,2,4,1,0:T(8,128)} %copy-done.1, f32[96,8,8,2]{0,2,3,1:T(8,128)S(1)} %get-tuple-element.300, pred[96,2,64]{0,2,1:T(8,128)(4,1)S(1)} %copy.135, bf16[2,64,8,128,1]{3,2,1,0,4:T(8,128)(2,1)S(1)} %bitcast_bitcast_fusion.5), kind=kOutput, calls=%fused_computation.1.clone.1 | convolution fusion | flops 206831616 | bytes 6664192 | tf_op jit(solution)/shard_map/while/body/eval_jaxpr/rkgpo,pokd->rkgpd/dot_general | solution.py:59
  221.2 2.8 fusion.61
  224.1 1.9 copy-done.1
  226.0 2.7 fusion.62
  230.4 4.9 %fusion.64 = f32[96,8,8,128]{3,0,2,1:T(8,128)S(1)} fusion(f32[96,8,8,2]{0,2,3,1:T(8,128)S(1)} %get-tuple-element.305, f32[8,2,64,96,8]{3,2,4,1,0:T(8,128)} %copy-done.1, f32[96,8,8,2]{0,2,3,1:T(8,128)S(1)} %get-tuple-element.300, pred[96,2,64]{0,2,1:T(8,128)(4,1)S(1)} %copy.135, bf16[2,64,8,128,1]{3,2,1,0,4:T(8,128)(2,1)S(1)} %bitcast_bitcast_fusion.5), kind=kOutput, calls=%fused_computation.1.clone.1 | convolution fusion | flops 206831616 | bytes 6664192 | tf_op jit(solution)/shard_map/while/body/eval_jaxpr/rkgpo,pokd->rkgpd/dot_general | solution.py:59
  236.8 11.8 %all_to_all.57 = f32[1,96,8,8]{1,3,0,2:T(8,128)S(1)} all-to-all(f32[1,96,8,8]{1,3,0,2:T(8,128)S(1)} %bitcast.172), channel_id=1, replica_groups=mesh['ctx'=8,'fsdp'=32] {'ctx'}, dimensions={2} | all-to-all | bytes 49152 | tf_op jit(solution)/shard_map/all_to_all | solution.py:98
  248.6 5.5 %all-to-all-start.2 = ((f32[1,96,8,8]{1,3,0,2:T(8,128)}), f32[1,96,8,8]{1,3,0,2:T(8,128)S(1)}, u32[]{:S(2)}, u32[]{:S(2)}) async-start(f32[1,96,8,8]{1,3,0,2:T(8,128)} %bitcast.177), calls=%async_computation.2 | async-start | bytes 65536 | tf_op jit(solution)/shard_map/all_to_all | solution.py:99
  254.2 3.4 copy.127
  257.6 1.9 all-to-all-done.2
  259.6 6.0 %all-to-all-start = ((f32[1,96,8,8,128]{4,3,1,0,2:T(8,128)}), f32[1,96,8,8,128]{4,3,1,0,2:T(8,128)S(1)}, u32[]{:S(2)}, u32[]{:S(2)}) async-start(f32[1,96,8,8,128]{4,3,1,0,2:T(8,128)} %bitcast.171), calls=%async_computation | async-start | bytes 6291456 | tf_op jit(solution)/shard_map/all_to_all | solution.py:97
  272.4 31.6 %all-to-all-done = f32[1,96,8,8,128]{4,3,1,0,2:T(8,128)S(1)} async-done(((f32[1,96,8,8,128]{4,3,1,0,2:T(8,128)}), f32[1,96,8,8,128]{4,3,1,0,2:T(8,128)S(1)}, u32[]{:S(2)}, u32[]{:S(2)}) %all-to-all-start) | async-done | bytes 3145760 | tf_op jit(solution)/shard_map/all_to_all | solution.py:97
  304.1 1.9 fusion.20
  306.6 10.5 %fusion.25 = f32[96,8192]{1,0:T(8,128)} fusion(bf16[1024,8192]{1,0:T(8,128)(2,1)} %all-gather.2.cloned.1.call-done, f32[12,8,8,128]{3,2,1,0:T(8,128)S(1)} %bitcast.176, f32[12,8,8,128]{3,2,1,0:T(8,128)S(1)} %bitcast.175, f32[12,8,8,128]{3,2,1,0:T(8,128)} %bitcast.178, f32[12,8,8,128]{3,2,1,0:T(8,128)S(1)} %bitcast.174), kind=kOutput, calls=%fused_computation.44 | convolution fusion | flops 1611005952 | bytes 21495808 | tf_op jit(solution)/shard_map/dot_general | solution.py:128
  317.1 85.3 %reduce-scatter.2.cloned.1.call-done = f32[96,1024]{1,0:T(8,128)} async-done(((f32[96,8192]{1,0:T(8,128)}), f32[96,1024]{1,0:T(8,128)}) %reduce-scatter.2.cloned.1.call-update) | async-done | bytes 393232 | tf_op jit(solution)/shard_map/reduce_scatter | solution.py:133
  (290 shorter events, 74.8 us)
Async XLA Ops:
  6.5 263.3 %copy-start = (bf16[24,4,1,128]{3,1,2,0:T(4,128)(2,1)S(1)}, bf16[24,4,1,128]{3,1,2,0:T(4,128)(2,1)}, u32[]{:S(2)}) copy-start(bf16[24,4,1,128]{3,1,2,0:T(4,128)(2,1)} %param.15) | copy-start | bytes 73732
  6.5 299.7 %all-gather.2.cloned.1.call-start = ((), (), s32[]{:S(2)}) async-start(), calls=%async_computation.4 | async-start | bytes 17301504 | tf_op jit(solution)/shard_map/all_gather | solution.py:130
  8.3 8.0 %copy-start.6 = (s32[24]{0:T(128)S(1)}, s32[24]{0:T(128)}, u32[]{:S(2)}) copy-start(s32[24]{0:T(128)} %param.17) | copy-start | bytes 292
  17.1 237.0 %copy-start.5 = (s32[24,4]{0,1:T(4,128)S(1)}, s32[24,4]{0,1:T(4,128)}, u32[]{:S(2)}) copy-start(s32[24,4]{0,1:T(4,128)} %param.18) | copy-start | bytes 1156
  22.6 1.9 copy-start.1
  22.6 6.2 %copy-start.2 = (bf16[2,64,1024]{2,1,0:T(8,128)(2,1)S(1)}, bf16[2,64,1024]{2,1,0:T(8,128)(2,1)}, u32[]{:S(2)}) copy-start(bf16[2,64,1024]{2,1,0:T(8,128)(2,1)} %get-tuple-element.306) | copy-start | bytes 786436 | tf_op jit(solution)/shard_map/while
  29.0 4.9 %copy-start.3 = (f32[96,8,8]{0,2,1:T(8,128)S(1)}, f32[96,8,8]{0,2,1:T(8,128)}, u32[]{:S(2)}) copy-start(f32[96,8,8]{0,2,1:T(8,128)} %get-tuple-element.322) | copy-start | bytes 73732 | tf_op jit(solution)/shard_map/while
  33.9 1.4 copy-start.4
  40.9 1.9 copy-start.1
  40.9 6.2 %copy-start.2 = (bf16[2,64,1024]{2,1,0:T(8,128)(2,1)S(1)}, bf16[2,64,1024]{2,1,0:T(8,128)(2,1)}, u32[]{:S(2)}) copy-start(bf16[2,64,1024]{2,1,0:T(8,128)(2,1)} %get-tuple-element.306) | copy-start | bytes 786436 | tf_op jit(solution)/shard_map/while
  47.2 5.0 %copy-start.3 = (f32[96,8,8]{0,2,1:T(8,128)S(1)}, f32[96,8,8]{0,2,1:T(8,128)}, u32[]{:S(2)}) copy-start(f32[96,8,8]{0,2,1:T(8,128)} %get-tuple-element.322) | copy-start | bytes 73732 | tf_op jit(solution)/shard_map/while
  52.3 1.4 copy-start.4
  59.4 1.9 copy-start.1
  59.4 6.3 %copy-start.2 = (bf16[2,64,1024]{2,1,0:T(8,128)(2,1)S(1)}, bf16[2,64,1024]{2,1,0:T(8,128)(2,1)}, u32[]{:S(2)}) copy-start(bf16[2,64,1024]{2,1,0:T(8,128)(2,1)} %get-tuple-element.306) | copy-start | bytes 786436 | tf_op jit(solution)/shard_map/while
  65.8 4.9 %copy-start.3 = (f32[96,8,8]{0,2,1:T(8,128)S(1)}, f32[96,8,8]{0,2,1:T(8,128)}, u32[]{:S(2)}) copy-start(f32[96,8,8]{0,2,1:T(8,128)} %get-tuple-element.322) | copy-start | bytes 73732 | tf_op jit(solution)/shard_map/while
  70.7 1.4 copy-start.4
  77.7 1.9 copy-start.1
  77.7 6.3 %copy-start.2 = (bf16[2,64,1024]{2,1,0:T(8,128)(2,1)S(1)}, bf16[2,64,1024]{2,1,0:T(8,128)(2,1)}, u32[]{:S(2)}) copy-start(bf16[2,64,1024]{2,1,0:T(8,128)(2,1)} %get-tuple-element.306) | copy-start | bytes 786436 | tf_op jit(solution)/shard_map/while
  84.1 4.9 %copy-start.3 = (f32[96,8,8]{0,2,1:T(8,128)S(1)}, f32[96,8,8]{0,2,1:T(8,128)}, u32[]{:S(2)}) copy-start(f32[96,8,8]{0,2,1:T(8,128)} %get-tuple-element.322) | copy-start | bytes 73732 | tf_op jit(solution)/shard_map/while
  89.0 1.4 copy-start.4
  96.0 1.9 copy-start.1
  96.0 6.3 %copy-start.2 = (bf16[2,64,1024]{2,1,0:T(8,128)(2,1)S(1)}, bf16[2,64,1024]{2,1,0:T(8,128)(2,1)}, u32[]{:S(2)}) copy-start(bf16[2,64,1024]{2,1,0:T(8,128)(2,1)} %get-tuple-element.306) | copy-start | bytes 786436 | tf_op jit(solution)/shard_map/while
  102.4 4.9 %copy-start.3 = (f32[96,8,8]{0,2,1:T(8,128)S(1)}, f32[96,8,8]{0,2,1:T(8,128)}, u32[]{:S(2)}) copy-start(f32[96,8,8]{0,2,1:T(8,128)} %get-tuple-element.322) | copy-start | bytes 73732 | tf_op jit(solution)/shard_map/while
  107.3 1.4 copy-start.4
  114.3 1.9 copy-start.1
  114.3 6.2 %copy-start.2 = (bf16[2,64,1024]{2,1,0:T(8,128)(2,1)S(1)}, bf16[2,64,1024]{2,1,0:T(8,128)(2,1)}, u32[]{:S(2)}) copy-start(bf16[2,64,1024]{2,1,0:T(8,128)(2,1)} %get-tuple-element.306) | copy-start | bytes 786436 | tf_op jit(solution)/shard_map/while
  120.7 5.0 %copy-start.3 = (f32[96,8,8]{0,2,1:T(8,128)S(1)}, f32[96,8,8]{0,2,1:T(8,128)}, u32[]{:S(2)}) copy-start(f32[96,8,8]{0,2,1:T(8,128)} %get-tuple-element.322) | copy-start | bytes 73732 | tf_op jit(solution)/shard_map/while
  125.7 1.4 copy-start.4
  132.7 1.9 copy-start.1
  132.7 6.2 %copy-start.2 = (bf16[2,64,1024]{2,1,0:T(8,128)(2,1)S(1)}, bf16[2,64,1024]{2,1,0:T(8,128)(2,1)}, u32[]{:S(2)}) copy-start(bf16[2,64,1024]{2,1,0:T(8,128)(2,1)} %get-tuple-element.306) | copy-start | bytes 786436 | tf_op jit(solution)/shard_map/while
  139.1 4.9 %copy-start.3 = (f32[96,8,8]{0,2,1:T(8,128)S(1)}, f32[96,8,8]{0,2,1:T(8,128)}, u32[]{:S(2)}) copy-start(f32[96,8,8]{0,2,1:T(8,128)} %get-tuple-element.322) | copy-start | bytes 73732 | tf_op jit(solution)/shard_map/while
  144.0 1.4 copy-start.4
  151.0 1.9 copy-start.1
  151.0 6.2 %copy-start.2 = (bf16[2,64,1024]{2,1,0:T(8,128)(2,1)S(1)}, bf16[2,64,1024]{2,1,0:T(8,128)(2,1)}, u32[]{:S(2)}) copy-start(bf16[2,64,1024]{2,1,0:T(8,128)(2,1)} %get-tuple-element.306) | copy-start | bytes 786436 | tf_op jit(solution)/shard_map/while
  157.3 4.9 %copy-start.3 = (f32[96,8,8]{0,2,1:T(8,128)S(1)}, f32[96,8,8]{0,2,1:T(8,128)}, u32[]{:S(2)}) copy-start(f32[96,8,8]{0,2,1:T(8,128)} %get-tuple-element.322) | copy-start | bytes 73732 | tf_op jit(solution)/shard_map/while
  162.2 1.4 copy-start.4
  169.3 1.9 copy-start.1
  169.3 6.2 %copy-start.2 = (bf16[2,64,1024]{2,1,0:T(8,128)(2,1)S(1)}, bf16[2,64,1024]{2,1,0:T(8,128)(2,1)}, u32[]{:S(2)}) copy-start(bf16[2,64,1024]{2,1,0:T(8,128)(2,1)} %get-tuple-element.306) | copy-start | bytes 786436 | tf_op jit(solution)/shard_map/while
  175.6 4.9 %copy-start.3 = (f32[96,8,8]{0,2,1:T(8,128)S(1)}, f32[96,8,8]{0,2,1:T(8,128)}, u32[]{:S(2)}) copy-start(f32[96,8,8]{0,2,1:T(8,128)} %get-tuple-element.322) | copy-start | bytes 73732 | tf_op jit(solution)/shard_map/while
  180.5 1.4 copy-start.4
  187.5 1.9 copy-start.1
  187.5 6.2 %copy-start.2 = (bf16[2,64,1024]{2,1,0:T(8,128)(2,1)S(1)}, bf16[2,64,1024]{2,1,0:T(8,128)(2,1)}, u32[]{:S(2)}) copy-start(bf16[2,64,1024]{2,1,0:T(8,128)(2,1)} %get-tuple-element.306) | copy-start | bytes 786436 | tf_op jit(solution)/shard_map/while
  193.9 4.9 %copy-start.3 = (f32[96,8,8]{0,2,1:T(8,128)S(1)}, f32[96,8,8]{0,2,1:T(8,128)}, u32[]{:S(2)}) copy-start(f32[96,8,8]{0,2,1:T(8,128)} %get-tuple-element.322) | copy-start | bytes 73732 | tf_op jit(solution)/shard_map/while
  198.8 1.4 copy-start.4
  205.8 1.9 copy-start.1
  205.8 6.2 %copy-start.2 = (bf16[2,64,1024]{2,1,0:T(8,128)(2,1)S(1)}, bf16[2,64,1024]{2,1,0:T(8,128)(2,1)}, u32[]{:S(2)}) copy-start(bf16[2,64,1024]{2,1,0:T(8,128)(2,1)} %get-tuple-element.306) | copy-start | bytes 786436 | tf_op jit(solution)/shard_map/while
  212.1 4.9 %copy-start.3 = (f32[96,8,8]{0,2,1:T(8,128)S(1)}, f32[96,8,8]{0,2,1:T(8,128)}, u32[]{:S(2)}) copy-start(f32[96,8,8]{0,2,1:T(8,128)} %get-tuple-element.322) | copy-start | bytes 73732 | tf_op jit(solution)/shard_map/while
  217.0 1.4 copy-start.4
  224.1 1.9 copy-start.1
  224.1 6.2 %copy-start.2 = (bf16[2,64,1024]{2,1,0:T(8,128)(2,1)S(1)}, bf16[2,64,1024]{2,1,0:T(8,128)(2,1)}, u32[]{:S(2)}) copy-start(bf16[2,64,1024]{2,1,0:T(8,128)(2,1)} %get-tuple-element.306) | copy-start | bytes 786436 | tf_op jit(solution)/shard_map/while
  230.4 4.9 %copy-start.3 = (f32[96,8,8]{0,2,1:T(8,128)S(1)}, f32[96,8,8]{0,2,1:T(8,128)}, u32[]{:S(2)}) copy-start(f32[96,8,8]{0,2,1:T(8,128)} %get-tuple-element.322) | copy-start | bytes 73732 | tf_op jit(solution)/shard_map/while
  235.3 1.4 copy-start.4
  248.6 11.0 %all-to-all-start.2 = ((f32[1,96,8,8]{1,3,0,2:T(8,128)}), f32[1,96,8,8]{1,3,0,2:T(8,128)S(1)}, u32[]{:S(2)}, u32[]{:S(2)}) async-start(f32[1,96,8,8]{1,3,0,2:T(8,128)} %bitcast.177), calls=%async_computation.2 | async-start | bytes 65536 | tf_op jit(solution)/shard_map/all_to_all | solution.py:99
  259.6 8.9 %copy-start.7 = (bf16[24,4,1,128]{3,1,2,0:T(4,128)(2,1)S(1)}, bf16[24,4,1,128]{3,1,2,0:T(4,128)(2,1)}, u32[]{:S(2)}) copy-start(bf16[24,4,1,128]{3,1,2,0:T(4,128)(2,1)} %param.14) | copy-start | bytes 73732
  259.6 44.5 %all-to-all-start = ((f32[1,96,8,8,128]{4,3,1,0,2:T(8,128)}), f32[1,96,8,8,128]{4,3,1,0,2:T(8,128)S(1)}, u32[]{:S(2)}, u32[]{:S(2)}) async-start(f32[1,96,8,8,128]{4,3,1,0,2:T(8,128)} %bitcast.171), calls=%async_computation | async-start | bytes 6291456 | tf_op jit(solution)/shard_map/all_to_all | solution.py:97
  265.5 136.8 %reduce-scatter.2.cloned.1.call-start = ((), (), s32[]{:S(2)}) async-start(), calls=%async_computation.5 | async-start | bytes 3538944 | tf_op jit(solution)/shard_map/reduce_scatter | solution.py:133
Sparse Core Ops, SparseCore 0:
  9.1 127.0 all-gather.1
  317.2 85.0 reduce-scatter.1
where the time goes:
time: 416 us; the launch traced here: 411 us
  waiting for transfers between devices  120 us (29%)
  matrix products  105 us (25%)
  other arithmetic  75.6 us (18%)
  local copies, waits for them, and re-layouts  71.7 us (17%)
  between operations  13.6 us (3%)
  blocking collectives  11.8 us (3%)
  starting transfers between devices  11.5 us (3%)
    reduce_scatter x1, waiting for transfers between devices, shards(): lax.psum_scatter(partial_sum, 'ctx', scatter_dimension=1, tiled=True)  85.3 us
    dot_general x12, matrix products, page_step(): jnp.einsum('rkgpo,pokd->rkgpd', weights, values_step, preferred_element_t...  58.5 us
    dot_general x12, matrix products, page_step(): jnp.einsum('rkgd,pokd->rkgpo', query_heads, keys_step, preferred_element_...  34.1 us
    reduce_sum x12, other arithmetic, page_step(): block_sum = jnp.sum(expo, axis=-1)  32.4 us
    all_to_all x1, waiting for transfers between devices, shards(): lax.all_to_all(local_out[None], 'ctx', split_axis=2, concat_axis=0, tiled...  31.6 us
    while x132, local copies, waits for them, and re-layouts  24.2 us
    dynamic_slice x12, local copies, waits for them, and re-layouts, page_step(): lax.dynamic_slice_in_dim(value_pages, stride * turn, stride, 0)  21.4 us
    add x12, other arithmetic, page_step(): run_out * keep[..., None] + jnp.sum(block_out * factor[..., None], axis=-2)  17 us
  transfers between devices with their start and end apart: 4, of which 3 were waited for; matrix products, arithmetic and copies ran while one was open for 53% of the time, Pallas kernels for 0%

commit v1 on v0

v1 whole, which is shorter than its diff:
```python
import functools

import jax
import jax.numpy as jnp
from jax import lax
from jax.experimental import pallas as pl
from jax.experimental.pallas import tpu as pltpu
from jax.sharding import PartitionSpec as P

SHARE = 8
DEAD = -1e30
LOG2E = 1.4426950408889634


def attention_kernel(
    shared_entries,
    table_ref,
    lengths_ref,
    parents_ref,
    query_hbm,
    keys_hbm,
    values_hbm,
    new_keys_hbm,
    new_values_hbm,
    out_hbm,
    lse_ref,
    query_ref,
    group_ref,
    new_keys_ref,
    new_values_ref,
    acc_ref,
    max_ref,
    sum_ref,
    out_ref,
    keys_ref,
    values_ref,
    unit_ref,
    query_sem,
    new_sem,
    out_sem,
    key_sem,
    value_sem,
):
    table_len, traj = table_ref.shape
    new = parents_ref.shape[0]
    pages_local, page_len, width = keys_hbm.shape
    kv_count, head_size, lanes = acc_ref.shape
    rows = SHARE * new
    groups = traj // SHARE
    heads = lanes // rows
    slots = keys_ref.shape[0]
    ctx_index = lax.axis_index("ctx")
    first_page = ctx_index * pages_local
    scale = LOG2E / head_size**0.5

    query_copies = [
        pltpu.make_async_copy(
            query_hbm.at[pl.ds(group * SHARE, SHARE)],
            query_ref.at[pl.ds(group * SHARE, SHARE)],
            query_sem.at[group],
        )
        for group in range(groups)
    ]
    new_copies = [
        pltpu.make_async_copy(new_keys_hbm, new_keys_ref, new_sem.at[0]),
        pltpu.make_async_copy(new_values_hbm, new_values_ref, new_sem.at[1]),
    ]
    query_copies[0].start()
    for copy in new_copies + query_copies[1:]:
        copy.start()

    def entry_live(member, entry, count, owner, reach):
        page = table_ref[entry, owner] - first_page
        live = (page >= 0) & (page < pages_local) & (reach > entry * page_len)

        @pl.when(live)
        def _():
            unit_ref[0, count] = member
            unit_ref[1, count] = page
            unit_ref[2, count] = entry * page_len

        return count + live.astype(jnp.int32)

    def own_units(owner, count):
        reach = lengths_ref[owner]
        last = jnp.minimum((reach + page_len - 1) // page_len, table_len)
        return lax.fori_loop(
            shared_entries,
            last,
            lambda entry, count: entry_live(owner % SHARE, entry, count, owner, reach),
            count,
        )

    count = 0
    bounds = [0]
    for group in range(groups):
        reach = lengths_ref[group * SHARE]
        for member in range(1, SHARE):
            reach = jnp.maximum(reach, lengths_ref[group * SHARE + member])
        count = lax.fori_loop(
            0,
            jnp.minimum((reach + page_len - 1) // page_len, shared_entries),
            lambda entry, count: entry_live(-1, entry, count, group * SHARE, reach),
            count,
        )
        count = lax.fori_loop(group * SHARE, (group + 1) * SHARE, own_units, count)
        bounds.append(count)

    def fetch(unit):
        slot = unit % slots
        page = unit_ref[1, unit]
        return (
            pltpu.make_async_copy(keys_hbm.at[page], keys_ref.at[slot], key_sem.at[slot]),
            pltpu.make_async_copy(values_hbm.at[page], values_ref.at[slot], value_sem.at[slot]),
        )

    def start_fetch(unit):
        @pl.when(unit < count)
        def _():
            for copy in fetch(unit):
                copy.start()

    for ahead in range(slots - 1):
        start_fetch(ahead)

    lane = lax.broadcasted_iota(jnp.int32, (1, lanes), 1)
    lane_token = lane % rows
    lane_traj = lane_token // new
    sub = lax.broadcasted_iota(jnp.int32, (rows, lanes), 0)
    own_row = lax.broadcasted_iota(jnp.int32, (kv_count, lanes), 0) == ctx_index
    position = lax.broadcasted_iota(jnp.int32, (page_len, lanes), 0)

    def gather_queries(group, kv):
        parts = []
        for head in range(heads):
            column = (kv * heads + head) * head_size
            if not isinstance(column, int):
                column = pl.multiple_of(column, head_size)
            value = query_ref[group * SHARE : (group + 1) * SHARE, :, pl.ds(column, head_size)]
            parts.append(value.reshape(rows, head_size))
        return jnp.concatenate(parts, axis=0)

    def block(keys, values, query, live):
        scores = (
            lax.dot_general(
                keys, query, (((1,), (1,)), ((), ())), preferred_element_type=jnp.float32
            )
            * scale
        )
        scores = jnp.where(live, scores, DEAD)
        block_max = jnp.max(scores, axis=0, keepdims=True)
        expo = jnp.exp2(scores - jnp.maximum(block_max, 0.1 * DEAD))
        block_sum = jnp.sum(expo, axis=0, keepdims=True)
        block_out = lax.dot_general(
            values,
            expo.astype(jnp.bfloat16),
            (((0,), (0,)), ((), ())),
            preferred_element_type=jnp.float32,
        )
        return block_max, block_sum, block_out

    def new_block(group):
        bits = jnp.zeros((1, lanes), jnp.int32)
        for member in range(SHARE):
            seen = []
            for token in range(new):
                parent = parents_ref[token, group * SHARE + member]
                mask = jnp.int32(1 << token)
                for earlier in range(token):
                    mask = mask | jnp.where(parent == earlier, seen[earlier], 0)
                seen.append(mask)
                bits = jnp.where(lane_token == member * new + token, mask, bits)
        live = (sub // new == lane_traj) & (((bits >> (sub % new)) & 1) == 1)
        span = slice(group * SHARE, (group + 1) * SHARE)
        return block(
            new_keys_ref[span].reshape(rows, head_size),
            new_values_ref[span].reshape(rows, head_size),
            gather_queries(group, ctx_index),
            live,
        )

    def unit_step(group, unit):
        start_fetch(unit + slots - 1)
        slot = unit % slots
        member = unit_ref[0, unit]
        offset = unit_ref[2, unit]
        limit = jnp.zeros((1, lanes), jnp.int32)
        for each in range(SHARE):
            reach = jnp.where(
                (member < 0) | (member == each), lengths_ref[group * SHARE + each] - offset, 0
            )
            limit = jnp.where(lane_traj == each, reach, limit)
        live = position < limit
        for copy in fetch(unit):
            copy.wait()
        run_max = max_ref[...]
        run_sum = sum_ref[...]
        next_max = []
        next_sum = []
        for kv in range(kv_count):
            columns = slice(kv * head_size, (kv + 1) * head_size)
            block_max, block_sum, block_out = block(
                keys_ref[slot, :, columns],
                values_ref[slot, :, columns],
                group_ref[kv],
                live,
            )
            old_max = run_max[kv : kv + 1]
            new_max = jnp.maximum(old_max, block_max)
            keep = jnp.exp2(old_max - new_max)
            factor = jnp.exp2(block_max - new_max)
            next_max.append(new_max)
            next_sum.append(run_sum[kv : kv + 1] * keep + block_sum * factor)
            acc_ref[kv] = acc_ref[kv] * keep + block_out * factor
        max_ref[...] = jnp.concatenate(next_max, axis=0)
        sum_ref[...] = jnp.concatenate(next_sum, axis=0)

    def finish(group):
        total = sum_ref[...]
        some = total > 0.0
        safe = jnp.where(some, total, 1.0)
        inverse = jnp.where(some, 1.0 / safe, 0.0)
        lse = jnp.where(some, max_ref[...] + jnp.log2(safe), DEAD)
        for kv in range(kv_count):
            lse_ref[kv, group : group + 1] = lse[kv : kv + 1]
        return inverse

    out_copies = []
    for group in range(groups):
        query_copies[group].wait()
        if group == 0:
            for copy in new_copies:
                copy.wait()
        block_max, block_sum, block_out = new_block(group)
        max_ref[...] = jnp.where(own_row, block_max, DEAD)
        sum_ref[...] = jnp.where(own_row, block_sum, 0.0)
        busy = bounds[group + 1] > bounds[group]

        @pl.when(busy)
        def _():
            for kv in range(kv_count):
                group_ref[kv] = gather_queries(group, kv)
                acc_ref[kv] = jnp.zeros((head_size, lanes), jnp.float32)
            acc_ref[ctx_index] = block_out

            def step(unit, _):
                unit_step(group, unit)
                return 0

            lax.fori_loop(bounds[group], bounds[group + 1], step, 0)
            inverse = finish(group)
            for kv in range(kv_count):
                out_ref[group, kv] = (acc_ref[kv] * inverse[kv : kv + 1]).astype(jnp.bfloat16)

        @pl.when(jnp.logical_not(busy))
        def _():
            inverse = finish(group)
            own = jnp.sum(jnp.where(own_row, inverse, 0.0), axis=0, keepdims=True)
            for kv in range(kv_count):
                out_ref[group, kv] = jnp.zeros((head_size, lanes), jnp.bfloat16)
            out_ref[group, ctx_index] = (block_out * own).astype(jnp.bfloat16)

        copy = pltpu.make_async_copy(out_ref.at[group], out_hbm.at[:, group], out_sem.at[group])
        copy.start()
        out_copies.append(copy)
    for copy in out_copies:
        copy.wait()


def page_attention(table, lengths, parents, query, keys, values, new_keys, new_values):
    table_len, traj = table.shape
    new = parents.shape[0]
    head_size = new_keys.shape[-1]
    rows = SHARE * new
    groups = traj // SHARE
    pages, page_len, width = keys.shape
    kv_count = width // head_size
    heads = query.shape[2] // width
    lanes = rows * heads
    slots = 4
    units = traj * table_len
    smem = pl.BlockSpec(memory_space=pltpu.SMEM)
    vmem = pl.BlockSpec(memory_space=pltpu.VMEM)
    anywhere = pl.BlockSpec(memory_space=pl.ANY)
    bf16, f32, dma = jnp.bfloat16, jnp.float32, pltpu.SemaphoreType.DMA
    return pl.pallas_call(
        functools.partial(attention_kernel, table_len // 2),
        out_shape=(
            jax.ShapeDtypeStruct((kv_count, groups, head_size, lanes), bf16),
            jax.ShapeDtypeStruct((kv_count, 8, lanes), f32),
        ),
        in_specs=[smem, smem, smem] + [anywhere] * 5,
        out_specs=(anywhere, vmem),
        scratch_shapes=[
            pltpu.VMEM(query.shape, bf16),
            pltpu.VMEM((kv_count, lanes, head_size), bf16),
            pltpu.VMEM(new_keys.shape, bf16),
            pltpu.VMEM(new_values.shape, bf16),
            pltpu.VMEM((kv_count, head_size, lanes), f32),
            pltpu.VMEM((kv_count, lanes), f32),
            pltpu.VMEM((kv_count, lanes), f32),
            pltpu.VMEM((groups, kv_count, head_size, lanes), bf16),
            pltpu.VMEM((slots, page_len, width), bf16),
            pltpu.VMEM((slots, page_len, width), bf16),
            pltpu.SMEM((3, units), jnp.int32),
            dma((groups,)),
            dma((2,)),
            dma((groups,)),
            dma((slots,)),
            dma((slots,)),
        ],
        cost_estimate=pl.CostEstimate(
            flops=10**10, bytes_accessed=10**7, transcendentals=10**7
        ),
        compiler_params=pltpu.CompilerParams(vmem_limit_bytes=56 * 1024 * 1024),
    )(table, lengths, parents, query, keys, values, new_keys, new_values)


def attend(queries, keys, values, new_keys, new_values, table, lengths, parents):
    traj, new, _, head_size = new_keys.shape
    return page_attention(
        table.T,
        lengths,
        parents.T,
        queries,
        keys,
        values,
        new_keys.reshape(traj, new, head_size),
        new_values.reshape(traj, new, head_size),
    )


CTX_STEPS = ((2, 1), (2, 0), (1, 1), (3, 1), (0, 1), (1, 0), (3, 0))
MESH = pl.DeviceIdType.MESH


def project_kernel(
    near,
    part_hbm,
    lse_ref,
    weight_hbm,
    other_weight,
    out_ref,
    weights,
    part_own,
    part_in,
    lse_in,
    total,
    own_rows,
    pair_rows,
    far_rows,
    product,
    shard_in,
    summed,
    returned,
    final,
    own_sem,
    weight_sem,
    weight_sems,
    part_sems,
    lse_sems,
    ring_sems,
    shard_sems,
    return_sems,
    final_send,
    final_recv,
):
    count = lax.axis_size("ctx")
    c = lax.axis_index("ctx")
    f = lax.axis_index("fsdp")
    z, r = f // near, f % near
    groups, head_size, lanes = part_own.shape
    rows = own_rows.shape[0]
    half = rows // 2
    token_rows = rows // groups
    heads = lanes // token_rows
    shard = product.shape[2]
    steps = len(CTX_STEPS)

    def ctx_step(index, sign):
        dx, dy = CTX_STEPS[index]
        return ((c // 2 + count + sign * dx) % (count // 2)) * 2 + (c % 2 + dy) % 2

    def at_ctx(other):
        return (other, f)

    def at_z(step):
        return (c, ((z + count + step) % count) * near + r)

    barrier = pltpu.get_barrier_semaphore()
    for index in range(steps):
        pl.semaphore_signal(barrier, inc=1, device_id=at_ctx(ctx_step(index, 1)), device_id_type=MESH)
    for step in range(1, count):
        pl.semaphore_signal(barrier, inc=1, device_id=at_z(step), device_id_type=MESH)
    other_core = (c, z * near + r // 2 * 2 + (r + 1) % 2)
    pl.semaphore_signal(barrier, inc=1, device_id=other_core, device_id_type=MESH)
    pl.semaphore_wait(barrier, steps + count)

    sent = []

    def send(source, target, sems, index, device):
        copy = pltpu.make_async_remote_copy(
            src_ref=source,
            dst_ref=target,
            send_sem=sems.at[(0,) + index],
            recv_sem=sems.at[(1,) + index],
            device_id=device,
            device_id_type=MESH,
        )
        copy.start()
        sent.append(copy)
        return copy

    lse_copies = []
    part_copies = []
    for index in range(steps):
        other = ctx_step(index, 1)
        lse_copies.append(
            send(lse_ref.at[other], lse_in.at[index], lse_sems, (index,), at_ctx(other))
        )
    for index in range(steps):
        other = ctx_step(index, 1)
        part_copies.append(
            send(part_hbm.at[other], part_in.at[index], part_sems, (index,), at_ctx(other))
        )
    own_copy = pltpu.make_async_copy(part_hbm.at[c], part_own, own_sem)
    own_copy.start()
    weight_copy = pltpu.make_async_copy(weight_hbm, weights.at[0], weight_sem)
    weight_copy.start()
    other_copies = [
        send(weight_hbm, weights.at[1], weight_sems, (0,), other_core),
        send(other_weight, weights.at[2], weight_sems, (1,), other_core),
    ]
    for copy in lse_copies:
        copy.wait_recv()
    each_lse = [lse_ref[c]] + [lse_in[index] for index in range(steps)]
    top = functools.reduce(jnp.maximum, each_lse)
    weighing = [jnp.exp2(lse - top) for lse in each_lse]
    inverse = 1.0 / functools.reduce(jnp.add, weighing)
    weighing = [weight * inverse for weight in weighing]
    own_copy.wait()
    for group in range(groups):
        total[group] = part_own[group].astype(jnp.float32) * weighing[0][group : group + 1]
    for index in range(steps):
        part_copies[index].wait_recv()
        for group in range(groups):
            total[group] += (
                part_in[index, group].astype(jnp.float32) * weighing[index + 1][group : group + 1]
            )
    for group in range(groups):
        turned = total[group].T.astype(jnp.bfloat16)
        for head in range(heads):
            own_rows[
                group * token_rows : (group + 1) * token_rows,
                head * head_size : (head + 1) * head_size,
            ] = turned[head * token_rows : (head + 1) * token_rows]

    ring = {}

    def forward(way, distance, part):
        base = 0 if way == 0 else rows
        span = pl.ds(part * half, half)
        far_span = pl.ds(base + part * half, half)
        source = own_rows.at[span] if distance == 1 else pair_rows.at[distance - 2, far_span]
        target = far_rows.at[span] if distance == 4 else pair_rows.at[distance - 1, far_span]
        ring[way, distance, part] = send(
            source, target, ring_sems, (way, distance - 1, part), at_z(1 if way == 0 else -1)
        )

    for part in range(2):
        for way in range(2):
            forward(way, 1, part)

    weight_copy.wait()
    for copy in other_copies:
        copy.wait_recv()
    shard_copies = {}

    def project(stage, value, base):
        size = value.shape[0]
        for index, weight in enumerate(
            (weights.at[0], weights.at[1], other_weight, weights.at[2])
        ):
            block = (r // 2 + index // 2) % 2 * 2 + (r % 2 + index % 2) % 2
            result = jnp.dot(value, weight[...], preferred_element_type=jnp.float32)
            result = result.astype(jnp.bfloat16)
            product[block * 2, base : base + size] = result[:, :shard]
            product[block * 2 + 1, base : base + size] = result[:, shard:]
        span = pl.ds(base, size)
        for index in range(steps):
            other = ctx_step(index, 1)
            shard_copies[stage, index] = send(
                product.at[other, span],
                shard_in.at[index, span],
                shard_sems,
                (stage, index),
                at_ctx(other),
            )

    return_copies = {}
    final_copies = []

    def reduce_stage(stage, base, size):
        for index in range(steps):
            shard_copies[stage, index].wait_recv()
        value = product[c, base : base + size].astype(jnp.float32)
        for index in range(steps):
            value = value + shard_in[index, base : base + size].astype(jnp.float32)
        summed[base : base + size] = value.astype(jnp.bfloat16)

    def send_back(slot, step, base):
        return_copies[slot] = send(
            summed.at[pl.ds(base, rows)], returned.at[slot], return_sems, (slot,), at_z(step)
        )

    def place(slot, source, column):
        copy = pltpu.make_async_remote_copy(
            src_ref=source,
            dst_ref=final.at[c],
            send_sem=final_send.at[slot],
            recv_sem=final_recv.at[c],
            device_id=at_ctx(column),
            device_id_type=MESH,
        )
        final_copies.append((copy, column))

        @pl.when(column != c)
        def _():
            copy.start()

        @pl.when(column == c)
        def _():
            final[c] = source[...]

    def arrive(slot, column):
        return_copies[slot].wait_recv()
        place(slot, returned.at[slot], column)

    def finish(stage):
        if stage == 0:
            reduce_stage(0, 0, rows)
            place(0, summed.at[pl.ds(0, rows)], z)
        elif stage < 4:
            base = rows * (2 * stage - 1)
            reduce_stage(stage, base, 2 * rows)
            send_back(2 * stage - 1, -stage, base)
            send_back(2 * stage, stage, base + rows)
        else:
            reduce_stage(4, 7 * rows, rows)
            send_back(7, 4, 7 * rows)

    def settle(stage):
        if 0 < stage < 4:
            arrive(2 * stage - 1, (z + stage) % count)
            arrive(2 * stage, (z + count - stage) % count)
        elif stage == 4:
            arrive(7, (z + 4) % count)

    project(0, own_rows[...], 0)
    for distance in range(1, 4):
        for part in range(2):
            for way in range(2):
                ring[way, distance, part].wait_recv()
                if distance < 3 or part == way:
                    forward(way, distance + 1, part)
        project(distance, pair_rows[distance - 1], rows * (2 * distance - 1))
        finish(distance - 1)
        settle(distance - 2)
    for way in range(2):
        ring[way, 4, way].wait_recv()
    project(4, far_rows[...], 7 * rows)
    finish(3)
    settle(2)
    finish(4)
    settle(3)
    settle(4)

    for copy, column in final_copies:

        @pl.when(column != c)
        def _():
            copy.wait_send()

    for source in range(count):

        @pl.when(c != source)
        def _():
            pltpu.make_async_remote_copy(
                src_ref=final.at[source],
                dst_ref=final.at[source],
                send_sem=final_send.at[0],
                recv_sem=final_recv.at[source],
                device_id=at_ctx((c + 1) % count),
                device_id_type=MESH,
            ).wait_recv()

        out_ref[:, source * shard : (source + 1) * shard] = final[source]
    for copy in sent:
        copy.wait_send()


def project(part, lse, weight, other_weight, near):
    count, groups, head_size, lanes = part.shape
    width = weight.shape[0]
    rows = groups * lanes * head_size // width
    columns = near * weight.shape[1]
    shard = columns // count
    steps = len(CTX_STEPS)
    vmem = pl.BlockSpec(memory_space=pltpu.VMEM)
    anywhere = pl.BlockSpec(memory_space=pl.ANY)
    bf16, f32, dma = jnp.bfloat16, jnp.float32, pltpu.SemaphoreType.DMA
    return pl.pallas_call(
        functools.partial(project_kernel, near),
        out_shape=jax.ShapeDtypeStruct((rows, columns), bf16),
        in_specs=[anywhere, vmem, anywhere, vmem],
        out_specs=vmem,
        scratch_shapes=[
            pltpu.VMEM((near - 1,) + weight.shape, bf16),
            pltpu.VMEM((groups, head_size, lanes), bf16),
            pltpu.VMEM((steps, groups, head_size, lanes), bf16),
            pltpu.VMEM((steps, lse.shape[1], lanes), f32),
            pltpu.VMEM((groups, head_size, lanes), f32),
            pltpu.VMEM((rows, width), bf16),
            pltpu.VMEM((3, 2 * rows, width), bf16),
            pltpu.VMEM((rows, width), bf16),
            pltpu.VMEM((count, 8 * rows, shard), bf16),
            pltpu.VMEM((steps, 8 * rows, shard), bf16),
            pltpu.VMEM((8 * rows, shard), bf16),
            pltpu.VMEM((8, rows, shard), bf16),
            pltpu.VMEM((count, rows, shard), bf16),
            dma,
            dma,
            dma((2, 2)),
            dma((2, steps)),
            dma((2, steps)),
            dma((2, 2, 4, 2)),
            dma((2, 5, steps)),
            dma((2, 8)),
            dma((8,)),
            dma((count,)),
        ],
        compiler_params=pltpu.CompilerParams(
            collective_id=0, has_side_effects=True, vmem_limit_bytes=52 * 1024 * 1024
        ),
    )(part, lse, weight, other_weight)


def shards(
    queries, key_pages, value_pages, new_keys, new_values, page_table, lengths, parents, o_weight
):
    ctx_count = lax.axis_size("ctx")
    fsdp_count = lax.axis_size("fsdp")
    traj, new, _ = queries.shape
    near = fsdp_count // ctx_count
    other_weight = lax.ppermute(o_weight, "fsdp", [(at, at ^ 2) for at in range(fsdp_count)])
    part, lse = attend(
        queries, key_pages, value_pages, new_keys, new_values, page_table, lengths, parents
    )
    mixed = project(part, lse, o_weight, other_weight, near)
    return mixed.reshape(traj, new, -1)


def solution(mesh):
    placed = (
        P("fsdp", None, None),
        P("ctx", None, None),
        P("ctx", None, None),
        P("fsdp", None, "ctx", None),
        P("fsdp", None, "ctx", None),
        P("fsdp", None),
        P("fsdp"),
        P("fsdp", None),
        P("ctx", "fsdp"),
    )
    return jax.shard_map(
        shards, mesh=mesh, in_specs=placed, out_specs=P("fsdp", None, "ctx"), check_vma=False
    )
```

time: 416 us -> 83.4 us (0.20); the launches traced: 411 us -> 83.2 us
  waiting for transfers between devices: 120 us -> 6.35 us
  matrix products: 105 us -> 0 us
  other arithmetic: 75.6 us -> 0 us
  Pallas kernels: 0 us -> 74.8 us
  local copies, waits for them, and re-layouts: 71.7 us -> 1.6 us
  between operations: 13.6 us -> 0.02 us
  blocking collectives: 11.8 us -> 0 us
  starting transfers between devices: 11.5 us -> 0.45 us
    dot_general x27 -> x0, matrix products: 105 us -> none  [the longest x12 58.5 us: page_step(): jnp.einsum('rkgpo,pokd->rkgpd', weights, values_step, preferred_element_t...]
    reduce_scatter x1 -> x0, waiting for transfers between devices: 85.3 us -> none  [shards(): lax.psum_scatter(partial_sum, 'ctx', scatter_dimension=1, tiled=True)]
    pallas_call x0 -> x2, Pallas kernels: none -> 74.8 us  [the longest x1 67.7 us: project(): pl.pallas_call(functools.partial(project_kernel, near), out_shape=jax.Sha...]
    reduce_sum x31 -> x0, other arithmetic: 46.8 us -> none  [the longest x12 32.4 us: page_step(): block_sum = jnp.sum(expo, axis=-1)]
    all_to_all x2 -> x0, waiting for transfers between devices: 33.6 us -> none  [the longest x1 31.6 us: shards(): lax.all_to_all(local_out[None], 'ctx', split_axis=2, concat_axis=0, tiled...]
    dynamic_slice x25 -> x0, local copies, waits for them, and re-layouts: 30.8 us -> none  [the longest x12 21.4 us: page_step(): lax.dynamic_slice_in_dim(value_pages, stride * turn, stride, 0)]
    while x133 -> x0, local copies, waits for them, and re-layouts: 27.6 us -> none
    add x27 -> x0, other arithmetic: 17.3 us -> none  [the longest x12 17 us: page_step(): run_out * keep[..., None] + jnp.sum(block_out * factor[..., None], axis=-2)]
  transfers between devices with their start and end apart: 4 -> 1, of which waited for: 3 -> 1; matrix products, arithmetic and copies ran while one was open for 53% -> 0% of each run, Pallas kernels for 0% -> 8%
where the time goes in v1:
time: 83.4 us; the launch traced here: 83.2 us
  Pallas kernels  74.8 us (90%)
  waiting for transfers between devices  6.35 us (8%)
  local copies, waits for them, and re-layouts  1.6 us (2%)
    pallas_call x1, Pallas kernels, project(): pl.pallas_call(functools.partial(project_kernel, near), out_shape=jax.Sha...  67.7 us
    pallas_call x1, Pallas kernels, page_attention(): pl.pallas_call(functools.partial(attention_kernel, table_len // 2), out_s...  7.06 us
    ppermute x1, waiting for transfers between devices, shards(): lax.ppermute(o_weight, 'fsdp', [(at, at ^ 2) for at in range(fsdp_count)])  6.35 us
  transfers between devices with their start and end apart: 1, of which 1 were waited for; matrix products, arithmetic and copies ran while one was open for 0% of the time, Pallas kernels for 8%

profile of v1, /device:TPU:12, one launch (start us, length us, event | category | flops | bytes accessed | tf_op | source)
XLA Modules:
  0.0 83.2 jit_solution(12998852203423112256)
XLA Ops:
  0.0 0.4 collective-permute-start
  0.5 0.0 copy-start
  0.5 7.1 %shard_map.91 = (bf16[8,3,128,256]{3,2,1,0:T(8,128)(2,1)}, f32[8,8,256]{2,1,0:T(8,128)}) custom-call(s32[16,24]{1,0:T(8,128)} %bitcast.6, s32[24]{0:T(128)} %lengths_ref.1, s32[4,24]{1,0:T(4,128)} %bitcast.7, bf16[24,4,8192]{2,1,0:T(4,128)(2,1)} %query_hbm.1, bf16[24,64,1024]{2,1,0:T(8,128)(2,1)} %keys_hbm.1, bf16[24,64,1024]{2,1,0:T(8,128)(2,1)} %values_hbm.1, ...), custom_call_target="tpu_custom_call" | custom-call | flops 10000000000 | bytes 10000000 | tf_op jit(solution)/shard_map/pallas_call | solution.py:286
  7.5 6.4 %collective-permute-done.other_weight = bf16[1024,256]{1,0:T(8,128)(2,1)S(1)} collective-permute-done((bf16[1024,256]{1,0:T(8,128)(2,1)}, bf16[1024,256]{1,0:T(8,128)(2,1)S(1)}, u32[]{:S(2)}, u32[]{:S(2)}) %collective-permute-start) | collective-permute-done | bytes 524320 | tf_op jit(solution)/shard_map/ppermute | solution.py:655
  13.9 0.0 copy-done
  13.9 0.0 copy-start.1
  13.9 0.8 %copy-done.1 = f32[8,8,256]{2,1,0:T(8,128)S(1)} copy-done((f32[8,8,256]{2,1,0:T(8,128)S(1)}, f32[8,8,256]{2,1,0:T(8,128)}, u32[]{:S(2)}) %copy-start.1) | copy-done | bytes 65560
  14.7 67.7 %shard_map.92 = bf16[96,1024]{1,0:T(8,128)(2,1)S(1)} custom-call(bf16[8,3,128,256]{3,2,1,0:T(8,128)(2,1)} %get-tuple-element.7.part_hbm, f32[8,8,256]{2,1,0:T(8,128)S(1)} %copy-done.1, bf16[1024,256]{1,0:T(8,128)(2,1)S(1)} %copy-done, bf16[1024,256]{1,0:T(8,128)(2,1)S(1)} %collective-permute-done.other_weight), custom_call_target="tpu_custom_call" | custom-call | tf_op jit(solution)/shard_map/pallas_call | solution.py:612
  82.5 0.8 reshape.11
Async XLA Ops:
  0.0 13.9 %collective-permute-start = (bf16[1024,256]{1,0:T(8,128)(2,1)}, bf16[1024,256]{1,0:T(8,128)(2,1)S(1)}, u32[]{:S(2)}, u32[]{:S(2)}) collective-permute-start(bf16[1024,256]{1,0:T(8,128)(2,1)} %weight_hbm.1), channel_id=1, source_target_pairs={{0,2},{1,3},{2,0},{3,1},{4,6},{5,7},{6,4},{7,5},{8,10},{9,11},{10,... | collective-permute-start | bytes 1572872 | tf_op jit(solution)/shard_map/ppermute | solution.py:655
  0.5 13.4 %copy-start = (bf16[1024,256]{1,0:T(8,128)(2,1)S(1)}, bf16[1024,256]{1,0:T(8,128)(2,1)}, u32[]{:S(2)}) copy-start(bf16[1024,256]{1,0:T(8,128)(2,1)} %weight_hbm.1) | copy-start | bytes 1572868
  13.9 0.8 %copy-start.1 = (f32[8,8,256]{2,1,0:T(8,128)S(1)}, f32[8,8,256]{2,1,0:T(8,128)}, u32[]{:S(2)}) copy-start(f32[8,8,256]{2,1,0:T(8,128)} %get-tuple-element.8.lse_ref) | copy-start | bytes 196612

commit v2 on v1

v2 whole, which is shorter than its diff:
```python
import functools

import jax
import jax.numpy as jnp
from jax import lax
from jax.experimental import pallas as pl
from jax.experimental.pallas import tpu as pltpu
from jax.sharding import PartitionSpec as P

SHARE = 8
DEAD = -1e30
LOG2E = 1.4426950408889634


def attention_kernel(
    shared_entries,
    table_ref,
    lengths_ref,
    parents_ref,
    query_hbm,
    keys_hbm,
    values_hbm,
    new_keys_hbm,
    new_values_hbm,
    out_hbm,
    lse_ref,
    query_ref,
    group_ref,
    new_keys_ref,
    new_values_ref,
    acc_ref,
    max_ref,
    sum_ref,
    out_ref,
    keys_ref,
    values_ref,
    unit_ref,
    query_sem,
    new_sem,
    out_sem,
    key_sem,
    value_sem,
):
    table_len, traj = table_ref.shape
    new = parents_ref.shape[0]
    pages_local, page_len, width = keys_hbm.shape
    kv_count, head_size, lanes = acc_ref.shape
    rows = SHARE * new
    groups = traj // SHARE
    heads = lanes // rows
    slots = keys_ref.shape[0]
    ctx_index = lax.axis_index("ctx")
    first_page = ctx_index * pages_local
    scale = LOG2E / head_size**0.5

    query_copies = [
        pltpu.make_async_copy(
            query_hbm.at[pl.ds(group * SHARE, SHARE)],
            query_ref.at[pl.ds(group * SHARE, SHARE)],
            query_sem.at[group],
        )
        for group in range(groups)
    ]
    new_copies = [
        pltpu.make_async_copy(new_keys_hbm, new_keys_ref, new_sem.at[0]),
        pltpu.make_async_copy(new_values_hbm, new_values_ref, new_sem.at[1]),
    ]
    query_copies[0].start()
    for copy in new_copies + query_copies[1:]:
        copy.start()

    def entry_live(member, entry, count, owner, reach):
        page = table_ref[entry, owner] - first_page
        live = (page >= 0) & (page < pages_local) & (reach > entry * page_len)

        @pl.when(live)
        def _():
            unit_ref[0, count] = member
            unit_ref[1, count] = page
            unit_ref[2, count] = entry * page_len

        return count + live.astype(jnp.int32)

    def own_units(owner, count):
        reach = lengths_ref[owner]
        last = jnp.minimum((reach + page_len - 1) // page_len, table_len)
        return lax.fori_loop(
            shared_entries,
            last,
            lambda entry, count: entry_live(owner % SHARE, entry, count, owner, reach),
            count,
        )

    count = 0
    bounds = [0]
    for group in range(groups):
        reach = lengths_ref[group * SHARE]
        for member in range(1, SHARE):
            reach = jnp.maximum(reach, lengths_ref[group * SHARE + member])
        count = lax.fori_loop(
            0,
            jnp.minimum((reach + page_len - 1) // page_len, shared_entries),
            lambda entry, count: entry_live(-1, entry, count, group * SHARE, reach),
            count,
        )
        count = lax.fori_loop(group * SHARE, (group + 1) * SHARE, own_units, count)
        bounds.append(count)

    def fetch(unit):
        slot = unit % slots
        page = unit_ref[1, unit]
        return (
            pltpu.make_async_copy(keys_hbm.at[page], keys_ref.at[slot], key_sem.at[slot]),
            pltpu.make_async_copy(values_hbm.at[page], values_ref.at[slot], value_sem.at[slot]),
        )

    def start_fetch(unit):
        @pl.when(unit < count)
        def _():
            for copy in fetch(unit):
                copy.start()

    for ahead in range(slots - 1):
        start_fetch(ahead)

    lane = lax.broadcasted_iota(jnp.int32, (1, lanes), 1)
    lane_token = lane // (lanes // 2) * (rows // 2) + lane % (rows // 2)
    lane_traj = lane_token // new
    sub = lax.broadcasted_iota(jnp.int32, (rows, lanes), 0)
    own_row = lax.broadcasted_iota(jnp.int32, (kv_count, lanes), 0) == ctx_index
    position = lax.broadcasted_iota(jnp.int32, (page_len, lanes), 0)

    def gather_queries(group, kv):
        parts = []
        for head in range(heads):
            column = (kv * heads + head) * head_size
            if not isinstance(column, int):
                column = pl.multiple_of(column, head_size)
            value = query_ref[group * SHARE : (group + 1) * SHARE, :, pl.ds(column, head_size)]
            parts.append(value.reshape(rows, head_size))
        return jnp.concatenate(
            [part[: rows // 2] for part in parts] + [part[rows // 2 :] for part in parts], axis=0
        )

    def block(keys, values, query, live):
        scores = (
            lax.dot_general(
                keys, query, (((1,), (1,)), ((), ())), preferred_element_type=jnp.float32
            )
            * scale
        )
        scores = jnp.where(live, scores, DEAD)
        block_max = jnp.max(scores, axis=0, keepdims=True)
        expo = jnp.exp2(scores - jnp.maximum(block_max, 0.1 * DEAD))
        block_sum = jnp.sum(expo, axis=0, keepdims=True)
        block_out = lax.dot_general(
            values,
            expo.astype(jnp.bfloat16),
            (((0,), (0,)), ((), ())),
            preferred_element_type=jnp.float32,
        )
        return block_max, block_sum, block_out

    def new_block(group):
        bits = jnp.zeros((1, lanes), jnp.int32)
        for member in range(SHARE):
            seen = []
            for token in range(new):
                parent = parents_ref[token, group * SHARE + member]
                mask = jnp.int32(1 << token)
                for earlier in range(token):
                    mask = mask | jnp.where(parent == earlier, seen[earlier], 0)
                seen.append(mask)
                bits = jnp.where(lane_token == member * new + token, mask, bits)
        live = (sub // new == lane_traj) & (((bits >> (sub % new)) & 1) == 1)
        span = slice(group * SHARE, (group + 1) * SHARE)
        return block(
            new_keys_ref[span].reshape(rows, head_size),
            new_values_ref[span].reshape(rows, head_size),
            gather_queries(group, ctx_index),
            live,
        )

    def unit_step(group, unit):
        start_fetch(unit + slots - 1)
        slot = unit % slots
        member = unit_ref[0, unit]
        offset = unit_ref[2, unit]
        limit = jnp.zeros((1, lanes), jnp.int32)
        for each in range(SHARE):
            reach = jnp.where(
                (member < 0) | (member == each), lengths_ref[group * SHARE + each] - offset, 0
            )
            limit = jnp.where(lane_traj == each, reach, limit)
        live = position < limit
        for copy in fetch(unit):
            copy.wait()
        run_max = max_ref[...]
        run_sum = sum_ref[...]
        next_max = []
        next_sum = []
        for kv in range(kv_count):
            columns = slice(kv * head_size, (kv + 1) * head_size)
            block_max, block_sum, block_out = block(
                keys_ref[slot, :, columns],
                values_ref[slot, :, columns],
                group_ref[kv],
                live,
            )
            old_max = run_max[kv : kv + 1]
            new_max = jnp.maximum(old_max, block_max)
            keep = jnp.exp2(old_max - new_max)
            factor = jnp.exp2(block_max - new_max)
            next_max.append(new_max)
            next_sum.append(run_sum[kv : kv + 1] * keep + block_sum * factor)
            acc_ref[kv] = acc_ref[kv] * keep + block_out * factor
        max_ref[...] = jnp.concatenate(next_max, axis=0)
        sum_ref[...] = jnp.concatenate(next_sum, axis=0)

    def finish(group):
        total = sum_ref[...]
        some = total > 0.0
        safe = jnp.where(some, total, 1.0)
        inverse = jnp.where(some, 1.0 / safe, 0.0)
        lse = jnp.where(some, max_ref[...] + jnp.log2(safe), DEAD)
        for kv in range(kv_count):
            for half in range(2):
                row = half * groups + group
                lse_ref[kv, row : row + 1] = lse[
                    kv : kv + 1, half * (lanes // 2) : (half + 1) * (lanes // 2)
                ]
        return inverse

    def store(group, kv, value):
        for half in range(2):
            out_ref[group, kv, half] = value[
                :, half * (lanes // 2) : (half + 1) * (lanes // 2)
            ]

    out_copies = []
    for group in range(groups):
        query_copies[group].wait()
        if group == 0:
            for copy in new_copies:
                copy.wait()
        block_max, block_sum, block_out = new_block(group)
        max_ref[...] = jnp.where(own_row, block_max, DEAD)
        sum_ref[...] = jnp.where(own_row, block_sum, 0.0)
        busy = bounds[group + 1] > bounds[group]

        @pl.when(busy)
        def _():
            for kv in range(kv_count):
                group_ref[kv] = gather_queries(group, kv)
                acc_ref[kv] = jnp.zeros((head_size, lanes), jnp.float32)
            acc_ref[ctx_index] = block_out

            def step(unit, _):
                unit_step(group, unit)
                return 0

            lax.fori_loop(bounds[group], bounds[group + 1], step, 0)
            inverse = finish(group)
            for kv in range(kv_count):
                store(group, kv, (acc_ref[kv] * inverse[kv : kv + 1]).astype(jnp.bfloat16))

        @pl.when(jnp.logical_not(busy))
        def _():
            inverse = finish(group)
            own = jnp.sum(jnp.where(own_row, inverse, 0.0), axis=0, keepdims=True)
            for kv in range(kv_count):
                store(group, kv, jnp.zeros((head_size, lanes), jnp.bfloat16))
            store(group, ctx_index, (block_out * own).astype(jnp.bfloat16))

        copy = pltpu.make_async_copy(out_ref.at[group], out_hbm.at[:, :, group], out_sem.at[group])
        copy.start()
        out_copies.append(copy)
    for copy in out_copies:
        copy.wait()


def page_attention(table, lengths, parents, query, keys, values, new_keys, new_values):
    table_len, traj = table.shape
    new = parents.shape[0]
    head_size = new_keys.shape[-1]
    rows = SHARE * new
    groups = traj // SHARE
    pages, page_len, width = keys.shape
    kv_count = width // head_size
    heads = query.shape[2] // width
    lanes = rows * heads
    slots = 4
    units = traj * table_len
    smem = pl.BlockSpec(memory_space=pltpu.SMEM)
    vmem = pl.BlockSpec(memory_space=pltpu.VMEM)
    anywhere = pl.BlockSpec(memory_space=pl.ANY)
    bf16, f32, dma = jnp.bfloat16, jnp.float32, pltpu.SemaphoreType.DMA
    return pl.pallas_call(
        functools.partial(attention_kernel, table_len // 2),
        out_shape=(
            jax.ShapeDtypeStruct((kv_count, 2, groups, head_size, lanes // 2), bf16),
            jax.ShapeDtypeStruct((kv_count, 8, lanes // 2), f32),
        ),
        in_specs=[smem, smem, smem] + [anywhere] * 5,
        out_specs=(anywhere, vmem),
        scratch_shapes=[
            pltpu.VMEM(query.shape, bf16),
            pltpu.VMEM((kv_count, lanes, head_size), bf16),
            pltpu.VMEM(new_keys.shape, bf16),
            pltpu.VMEM(new_values.shape, bf16),
            pltpu.VMEM((kv_count, head_size, lanes), f32),
            pltpu.VMEM((kv_count, lanes), f32),
            pltpu.VMEM((kv_count, lanes), f32),
            pltpu.VMEM((groups, kv_count, 2, head_size, lanes // 2), bf16),
            pltpu.VMEM((slots, page_len, width), bf16),
            pltpu.VMEM((slots, page_len, width), bf16),
            pltpu.SMEM((3, units), jnp.int32),
            dma((groups,)),
            dma((2,)),
            dma((groups,)),
            dma((slots,)),
            dma((slots,)),
        ],
        cost_estimate=pl.CostEstimate(
            flops=10**10, bytes_accessed=10**7, transcendentals=10**7
        ),
        compiler_params=pltpu.CompilerParams(vmem_limit_bytes=56 * 1024 * 1024),
    )(table, lengths, parents, query, keys, values, new_keys, new_values)


def attend(queries, keys, values, new_keys, new_values, table, lengths, parents):
    traj, new, _, head_size = new_keys.shape
    return page_attention(
        table.T,
        lengths,
        parents.T,
        queries,
        keys,
        values,
        new_keys.reshape(traj, new, head_size),
        new_values.reshape(traj, new, head_size),
    )


CTX_STEPS = ((2, 1), (2, 0), (1, 1), (3, 1), (0, 1), (1, 0), (3, 0))
MESH = pl.DeviceIdType.MESH


def project_kernel(
    near,
    part_hbm,
    lse_hbm,
    weight_hbm,
    weight_below,
    weight_above,
    out_ref,
    weights,
    part_own,
    part_in,
    lse_own,
    lse_in,
    total,
    gathered,
    product,
    shard_in,
    summed,
    final,
    own_sems,
    part_sems,
    lse_sems,
    ring_sems,
    gather_sems,
    shard_sems,
    final_sems,
):
    count = lax.axis_size("ctx")
    c = lax.axis_index("ctx")
    f = lax.axis_index("fsdp")
    z, r = f // near, f % near
    halves, groups, head_size, lanes = part_own.shape
    rows = gathered.shape[2]
    token_rows = rows // groups
    heads = lanes // token_rows
    shard = product.shape[2]
    piece_rows = weights.shape[1] // 2
    steps = len(CTX_STEPS)

    def ctx_step(dx, dy):
        return ((c // 2 + dx) % (count // 2)) * 2 + (c % 2 + dy) % 2

    others = [ctx_step(*step) for step in CTX_STEPS]
    locals_ = [
        (r // 2 + dy) % 2 * 2 + (r % 2 + dcore) % 2 for dy, dcore in ((0, 1), (1, 0), (1, 1))
    ]

    def at_ctx(other):
        return (other, f)

    def at_local(other):
        return (c, z * near + other)

    def at_z(step):
        return (c, ((z + count + step) % count) * near + r)

    barrier = pltpu.get_barrier_semaphore()
    peers = [at_ctx(other) for other in others]
    peers += [at_z(1), at_z(-1)] + [at_local(other) for other in locals_]
    for peer in peers:
        pl.semaphore_signal(barrier, inc=1, device_id=peer, device_id_type=MESH)
    below, above = (z + count - 1) % count, (z + 1) % count
    own_copies = [
        pltpu.make_async_copy(source, target, own_sems.at[index])
        for index, (source, target) in enumerate(
            (
                (lse_hbm.at[c], lse_own),
                (part_hbm.at[c], part_own),
                (weight_hbm, weights.at[z]),
                (weight_below, weights.at[below]),
                (weight_above, weights.at[above]),
            )
        )
    ]
    for copy in own_copies:
        copy.start()
    pl.semaphore_wait(barrier, len(peers))

    def send(source, target, sems, index, device):
        copy = pltpu.make_async_remote_copy(
            src_ref=source,
            dst_ref=target,
            send_sem=sems.at[(0,) + index],
            recv_sem=sems.at[(1,) + index],
            device_id=device,
            device_id_type=MESH,
        )
        copy.start()
        return copy

    lse_copies = [
        send(lse_hbm.at[other], lse_in.at[index], lse_sems, (index,), at_ctx(other))
        for index, other in enumerate(others)
    ]

    def send_part(half, index):
        return send(
            part_hbm.at[others[index], half],
            part_in.at[index, half],
            part_sems,
            (index, half),
            at_ctx(others[index]),
        )

    ring = {}

    def forward(distance, part):
        for way in range(2):
            if distance == 4 and way != part:
                continue
            origin = (z + count + (1 - distance if way == 0 else distance - 1)) % count
            span = pl.ds(part * piece_rows, piece_rows)
            target = weights.at[origin, span]
            if distance == 2:
                source = (weight_below, weight_above)[way].at[span]
            else:
                source = target
            ring[distance, part, way] = send(
                source, target, ring_sems, (distance - 2, part, way), at_z(1 if way == 0 else -1)
            )

    def receive(distance, part):
        for way in range(2):
            if distance == 4 and way != part:
                continue
            ring[distance, part, way].wait_recv()
        if distance < 4:
            forward(distance + 1, part)

    part_copies = [[send_part(0, index) for index in range(steps)], []]
    forward(2, 0)
    forward(2, 1)
    for index in range(steps):
        part_copies[0][index].wait_send()
        part_copies[1].append(send_part(1, index))

    own_copies[0].wait()
    for copy in lse_copies:
        copy.wait_recv()
    each_lse = [lse_own[...]] + [lse_in[index] for index in range(steps)]
    top = functools.reduce(jnp.maximum, each_lse)
    weighing = [jnp.exp2(lse - top) for lse in each_lse]
    inverse = 1.0 / functools.reduce(jnp.add, weighing)
    weighing = [weight * inverse for weight in weighing]
    own_copies[1].wait()
    gathers = {}

    def combine(half):
        for group in range(groups):
            row = half * groups + group
            total[group] = part_own[half, group].astype(jnp.float32) * weighing[0][row : row + 1]
        for index in range(steps):
            part_copies[half][index].wait_recv()
            for group in range(groups):
                row = half * groups + group
                total[group] += (
                    part_in[index, half, group].astype(jnp.float32)
                    * weighing[index + 1][row : row + 1]
                )
        for group in range(groups):
            turned = total[group].T.astype(jnp.bfloat16)
            for head in range(heads):
                gathered[
                    half,
                    r,
                    group * token_rows : (group + 1) * token_rows,
                    head * head_size : (head + 1) * head_size,
                ] = turned[head * token_rows : (head + 1) * token_rows]
        for index in range(2):
            block = gathered.at[half, r]
            gathers[half, index] = send(
                block, block, gather_sems, (half, index), at_local(locals_[index])
            )

    def relay(half):
        gathers[half, 1].wait_recv()
        block = gathered.at[half, locals_[1]]
        gathers[half, 2] = send(block, block, gather_sems, (half, 2), at_local(locals_[0]))

    receive(2, 0)
    combine(0)
    receive(2, 1)
    relay(0)
    receive(3, 0)
    combine(1)
    relay(1)
    receive(3, 1)
    for half in range(halves):
        for index in (0, 2):
            gathers[half, index].wait_recv()
    for copy in own_copies[2:]:
        copy.wait()
    receive(4, 0)
    receive(4, 1)

    shard_copies = []

    def project(column):
        for half in range(halves):
            value = gathered[half].reshape(near * rows, weights.shape[1])
            result = jnp.dot(value, weights[column], preferred_element_type=jnp.float32)
            product[column, half * near * rows : (half + 1) * near * rows] = result.astype(
                jnp.bfloat16
            )

    for index, other in enumerate(others):
        project(other)
        shard_copies.append(
            send(product.at[other], shard_in.at[index], shard_sems, (index,), at_ctx(other))
        )
    project(c)
    for copy in shard_copies:
        copy.wait_recv()
    final_copies = []
    for index, owner in enumerate([*locals_[::-1], r]):
        for half in range(halves):
            base = pl.multiple_of((half * near + owner) * rows, rows)
            span = pl.ds(base, rows)
            value = product[c, span].astype(jnp.float32)
            for step in range(steps):
                value = value + shard_in[step, span].astype(jnp.float32)
            summed[owner, half] = value.astype(jnp.bfloat16)
        if index < near - 1:
            final_copies.append(
                send(summed.at[owner], final.at[r], final_sems, (index,), at_local(owner))
            )
    final[r] = summed[r]
    for copy in final_copies:
        copy.wait_recv()
    for source in range(near):
        for half in range(halves):
            for group in range(groups):
                start = (group * halves + half) * token_rows
                out_ref[start : start + token_rows, source * shard : (source + 1) * shard] = final[
                    source, half, group * token_rows : (group + 1) * token_rows
                ]
    started = lse_copies + part_copies[1] + shard_copies + final_copies
    for copies in (ring, gathers):
        started += copies.values()
    for copy in started:
        copy.wait_send()


def project(part, lse, weight, weight_below, weight_above, near):
    count, halves, groups, head_size, lanes = part.shape
    width, shard = weight.shape
    rows = groups * lanes * head_size // width
    steps = len(CTX_STEPS)
    vmem = pl.BlockSpec(memory_space=pltpu.VMEM)
    anywhere = pl.BlockSpec(memory_space=pl.ANY)
    bf16, f32, dma = jnp.bfloat16, jnp.float32, pltpu.SemaphoreType.DMA
    return pl.pallas_call(
        functools.partial(project_kernel, near),
        out_shape=jax.ShapeDtypeStruct((halves * rows, near * shard), bf16),
        in_specs=[anywhere, anywhere, anywhere, vmem, vmem],
        out_specs=vmem,
        scratch_shapes=[
            pltpu.VMEM((count,) + weight.shape, bf16),
            pltpu.VMEM((halves, groups, head_size, lanes), bf16),
            pltpu.VMEM((steps, halves, groups, head_size, lanes), bf16),
            pltpu.VMEM(lse.shape[1:], f32),
            pltpu.VMEM((steps,) + lse.shape[1:], f32),
            pltpu.VMEM((groups, head_size, lanes), f32),
            pltpu.VMEM((halves, near, rows, width), bf16),
            pltpu.VMEM((count, near * halves * rows, shard), bf16),
            pltpu.VMEM((steps, near * halves * rows, shard), bf16),
            pltpu.VMEM((near, halves, rows, shard), bf16),
            pltpu.VMEM((near, halves, rows, shard), bf16),
            dma((5,)),
            dma((2, steps, halves)),
            dma((2, steps)),
            dma((2, 3, 2, 2)),
            dma((2, halves, 3)),
            dma((2, steps)),
            dma((2, 3)),
        ],
        compiler_params=pltpu.CompilerParams(
            collective_id=0, has_side_effects=True, vmem_limit_bytes=51 * 1024 * 1024
        ),
    )(part, lse, weight, weight_below, weight_above)


def shards(
    queries, key_pages, value_pages, new_keys, new_values, page_table, lengths, parents, o_weight
):
    ctx_count = lax.axis_size("ctx")
    fsdp_count = lax.axis_size("fsdp")
    traj, new, _ = queries.shape
    near = fsdp_count // ctx_count

    def moved(step):
        pairs = [(at, (at + step * near) % fsdp_count) for at in range(fsdp_count)]
        return lax.ppermute(o_weight, "fsdp", pairs)

    weight_below, weight_above = moved(1), moved(-1)
    part, lse = attend(
        queries, key_pages, value_pages, new_keys, new_values, page_table, lengths, parents
    )
    mixed = project(part, lse, o_weight, weight_below, weight_above, near)
    return mixed.reshape(traj, new, -1)


def solution(mesh):
    placed = (
        P("fsdp", None, None),
        P("ctx", None, None),
        P("ctx", None, None),
        P("fsdp", None, "ctx", None),
        P("fsdp", None, "ctx", None),
        P("fsdp", None),
        P("fsdp"),
        P("fsdp", None),
        P("ctx", "fsdp"),
    )
    return jax.shard_map(
        shards, mesh=mesh, in_specs=placed, out_specs=P("fsdp", None, "ctx"), check_vma=False
    )
```

time: 83.4 us -> 84.3 us (1.011)
  the two profiles are of different devices: /device:TPU:12 before, /device:TPU:8 now
where the time goes in v2:
time: 84.3 us; the launch traced here: 84.1 us
  Pallas kernels  74 us (88%)
  starting transfers between devices  5.86 us (7%)
  waiting for transfers between devices  2.65 us (3%)
  local copies, waits for them, and re-layouts  1.52 us (2%)
    pallas_call x1, Pallas kernels, project(): pl.pallas_call(functools.partial(project_kernel, near), out_shape=jax.Sha...  64.6 us
    pallas_call x1, Pallas kernels, page_attention(): pl.pallas_call(functools.partial(attention_kernel, table_len // 2), out_s...  9.47 us
    ppermute x2, starting transfers between devices, moved(): return lax.ppermute(o_weight, 'fsdp', pairs)  5.86 us
    ppermute x2, waiting for transfers between devices, moved(): return lax.ppermute(o_weight, 'fsdp', pairs)  2.65 us
  transfers between devices with their start and end apart: 2, of which 1 were waited for; matrix products, arithmetic and copies ran while one was open for 0% of the time, Pallas kernels for 11%

profile of v2, /device:TPU:8, one launch (start us, length us, event | category | flops | bytes accessed | tf_op | source)
XLA Modules:
  0.0 84.1 jit_solution(13612316039744361529)
XLA Ops:
  0.0 1.9 %collective-permute-start = (bf16[1024,256]{1,0:T(8,128)(2,1)}, bf16[1024,256]{1,0:T(8,128)(2,1)S(1)}, u32[]{:S(2)}, u32[]{:S(2)}) collective-permute-start(bf16[1024,256]{1,0:T(8,128)(2,1)} %weight_hbm.1), channel_id=1, source_target_pairs={{0,4},{1,5},{2,6},{3,7},{4,8},{5,9},{6,10},{7,11},{8,12},{9,13},{1... | collective-permute-start | bytes 1572872 | tf_op jit(solution)/shard_map/ppermute | solution.py:641
  1.9 3.9 %collective-permute-start.1 = (bf16[1024,256]{1,0:T(8,128)(2,1)}, bf16[1024,256]{1,0:T(8,128)(2,1)S(1)}, u32[]{:S(2)}, u32[]{:S(2)}) collective-permute-start(bf16[1024,256]{1,0:T(8,128)(2,1)} %weight_hbm.1), channel_id=1, source_target_pairs={{0,28},{1,29},{2,30},{3,31},{4,0},{5,1},{6,2},{7,3},{8,4},{9,5},{1... | collective-permute-start | bytes 1572872 | tf_op jit(solution)/shard_map/ppermute | solution.py:641
  5.9 0.0 copy-start
  5.9 9.5 %shard_map.91 = (bf16[8,2,3,128,128]{4,3,2,1,0:T(8,128)(2,1)}, f32[8,8,128]{2,1,0:T(8,128)}) custom-call(s32[16,24]{1,0:T(8,128)} %bitcast.6, s32[24]{0:T(128)} %lengths_ref.1, s32[4,24]{1,0:T(4,128)} %bitcast.7, bf16[24,4,8192]{2,1,0:T(4,128)(2,1)} %query_hbm.1, bf16[24,64,1024]{2,1,0:T(8,128)(2,1)} %keys_hbm.1, bf16[24,64,1024]{2,1,0:T(8,128)(2,1)} %values_hbm.1, ...), custom_call_target="tpu_custom_call" | custom-call | flops 10000000000 | bytes 10000000 | tf_op jit(solution)/shard_map/pallas_call | solution.py:298
  15.3 2.6 %collective-permute-done.weight_below = bf16[1024,256]{1,0:T(8,128)(2,1)S(1)} collective-permute-done((bf16[1024,256]{1,0:T(8,128)(2,1)}, bf16[1024,256]{1,0:T(8,128)(2,1)S(1)}, u32[]{:S(2)}, u32[]{:S(2)}) %collective-permute-start) | collective-permute-done | bytes 524320 | tf_op jit(solution)/shard_map/ppermute | solution.py:641
  18.0 0.0 collective-permute-done.1.weight_above
  18.0 0.0 copy-done
  18.0 0.0 copy-start.1
  18.0 0.8 copy-done.1
  18.8 64.6 %shard_map.92 = bf16[96,1024]{1,0:T(8,128)(2,1)S(1)} custom-call(bf16[8,2,3,128,128]{4,3,2,1,0:T(8,128)(2,1)} %get-tuple-element.7.part_hbm, f32[8,8,128]{2,1,0:T(8,128)S(1)} %copy-done.1, bf16[1024,256]{1,0:T(8,128)(2,1)S(1)} %copy-done, bf16[1024,256]{1,0:T(8,128)(2,1)S(1)} %collective-permute-done.weight_below, ...), custom_call_target="tpu_custom_call" | custom-call | tf_op jit(solution)/shard_map/pallas_call | solution.py:600
  83.3 0.8 reshape.11
Async XLA Ops:
  0.0 18.0 %collective-permute-start = (bf16[1024,256]{1,0:T(8,128)(2,1)}, bf16[1024,256]{1,0:T(8,128)(2,1)S(1)}, u32[]{:S(2)}, u32[]{:S(2)}) collective-permute-start(bf16[1024,256]{1,0:T(8,128)(2,1)} %weight_hbm.1), channel_id=1, source_target_pairs={{0,4},{1,5},{2,6},{3,7},{4,8},{5,9},{6,10},{7,11},{8,12},{9,13},{1... | collective-permute-start | bytes 1572872 | tf_op jit(solution)/shard_map/ppermute | solution.py:641
  1.9 16.1 %collective-permute-start.1 = (bf16[1024,256]{1,0:T(8,128)(2,1)}, bf16[1024,256]{1,0:T(8,128)(2,1)S(1)}, u32[]{:S(2)}, u32[]{:S(2)}) collective-permute-start(bf16[1024,256]{1,0:T(8,128)(2,1)} %weight_hbm.1), channel_id=1, source_target_pairs={{0,28},{1,29},{2,30},{3,31},{4,0},{5,1},{6,2},{7,3},{8,4},{9,5},{1... | collective-permute-start | bytes 1572872 | tf_op jit(solution)/shard_map/ppermute | solution.py:641
  5.9 12.1 %copy-start = (bf16[1024,256]{1,0:T(8,128)(2,1)S(1)}, bf16[1024,256]{1,0:T(8,128)(2,1)}, u32[]{:S(2)}) copy-start(bf16[1024,256]{1,0:T(8,128)(2,1)} %weight_hbm.1) | copy-start | bytes 1572868
  18.0 0.8 copy-start.1

commit v3 on v2

--- a/solution.py
+++ b/solution.py
@@ -363,15 +363,13 @@
     gathered,
     product,
     shard_in,
-    summed,
-    final,
     own_sems,
     part_sems,
     lse_sems,
     ring_sems,
     gather_sems,
-    shard_sems,
-    final_sems,
+    shard_send,
+    shard_recv,
 ):
     count = lax.axis_size("ctx")
     c = lax.axis_index("ctx")
@@ -381,7 +379,7 @@
     rows = gathered.shape[2]
     token_rows = rows // groups
     heads = lanes // token_rows
-    shard = product.shape[2]
+    shard = product.shape[4]
     piece_rows = weights.shape[1] // 2
     steps = len(CTX_STEPS)
 
@@ -403,8 +401,8 @@
         return (c, ((z + count + step) % count) * near + r)
 
     barrier = pltpu.get_barrier_semaphore()
-    peers = [at_ctx(other) for other in others]
-    peers += [at_z(1), at_z(-1)] + [at_local(other) for other in locals_]
+    peers = [at_ctx(other) for other in others] + [at_z(1), at_z(-1)]
+    peers += [(other, z * near + local) for local in locals_ for other in (*others, c)]
     for peer in peers:
         pl.semaphore_signal(barrier, inc=1, device_id=peer, device_id_type=MESH)
     below, above = (z + count - 1) % count, (z + 1) % count
@@ -538,51 +536,75 @@
             gathers[half, index].wait_recv()
     for copy in own_copies[2:]:
         copy.wait()
-    receive(4, 0)
-    receive(4, 1)
 
     shard_copies = []
 
-    def project(column):
+    def project(turn):
+        far_turn = 3 + c % (count - 3)
+        nearer = turn - (turn > far_turn).astype(jnp.int32)
+        column = jnp.where(
+            turn == far_turn, z + count // 2, z + count - 3 + (c + nearer) % (count - 1)
+        )
+        column = lax.rem(column, count)
         for half in range(halves):
             value = gathered[half].reshape(near * rows, weights.shape[1])
             result = jnp.dot(value, weights[column], preferred_element_type=jnp.float32)
-            product[column, half * near * rows : (half + 1) * near * rows] = result.astype(
-                jnp.bfloat16
+            result = result.astype(jnp.bfloat16)
+            for owner in range(near):
+                product[column, owner, half] = result[owner * rows : (owner + 1) * rows]
+        for index, owner in enumerate([*locals_[::-1], r]):
+            copy = pltpu.make_async_remote_copy(
+                src_ref=product.at[column, owner],
+                dst_ref=shard_in.at[c, r],
+                send_sem=shard_send.at[turn, index],
+                recv_sem=shard_recv.at[c, r],
+                device_id=(column, z * near + owner),
+                device_id_type=MESH,
             )
-
-    for index, other in enumerate(others):
-        project(other)
-        shard_copies.append(
-            send(product.at[other], shard_in.at[index], shard_sems, (index,), at_ctx(other))
-        )
-    project(c)
-    for copy in shard_copies:
-        copy.wait_recv()
-    final_copies = []
-    for index, owner in enumerate([*locals_[::-1], r]):
-        for half in range(halves):
-            base = pl.multiple_of((half * near + owner) * rows, rows)
-            span = pl.ds(base, rows)
-            value = product[c, span].astype(jnp.float32)
-            for step in range(steps):
-                value = value + shard_in[step, span].astype(jnp.float32)
-            summed[owner, half] = value.astype(jnp.bfloat16)
-        if index < near - 1:
-            final_copies.append(
-                send(summed.at[owner], final.at[r], final_sems, (index,), at_local(owner))
-            )
-    final[r] = summed[r]
-    for copy in final_copies:
-        copy.wait_recv()
+            remote = True if index < near - 1 else column != c
+            shard_copies.append((copy, remote))
+
+            @pl.when(remote)
+            def _():
+                copy.start()
+
+    for turn in range(count):
+        if turn == 3:
+            receive(4, 0)
+            receive(4, 1)
+        project(jnp.int32(turn))
+    shard_in[c, r] = product[c, r]
     for source in range(near):
+        for other in range(count):
+
+            @pl.when((other != c) | (source != r))
+            def _():
+                pltpu.make_async_remote_copy(
+                    src_ref=shard_in.at[other, source],
+                    dst_ref=shard_in.at[other, source],
+                    send_sem=shard_send.at[0, 0],
+                    recv_sem=shard_recv.at[other, source],
+                    device_id=at_z(1),
+                    device_id_type=MESH,
+                ).wait_recv()
+
+        value = shard_in[0, source].astype(jnp.float32)
+        for other in range(1, count):
+            value = value + shard_in[other, source].astype(jnp.float32)
+        value = value.astype(jnp.bfloat16)
         for half in range(halves):
             for group in range(groups):
                 start = (group * halves + half) * token_rows
-                out_ref[start : start + token_rows, source * shard : (source + 1) * shard] = final[
-                    source, half, group * token_rows : (group + 1) * token_rows
+                out_ref[start : start + token_rows, source * shard : (source + 1) * shard] = value[
+                    half, group * token_rows : (group + 1) * token_rows
                 ]
-    started = lse_copies + part_copies[1] + shard_copies + final_copies
+    for copy, remote in shard_copies:
+
+        @pl.when(remote)
+        def _():
+            copy.wait_send()
+
+    started = lse_copies + part_copies[1]
     for copies in (ring, gathers):
         started += copies.values()
     for copy in started:
@@ -610,17 +632,15 @@
             pltpu.VMEM((steps,) + lse.shape[1:], f32),
             pltpu.VMEM((groups, head_size, lanes), f32),
             pltpu.VMEM((halves, near, rows, width), bf16),
-            pltpu.VMEM((count, near * halves * rows, shard), bf16),
-            pltpu.VMEM((steps, near * halves * rows, shard), bf16),
-            pltpu.VMEM((near, halves, rows, shard), bf16),
-            pltpu.VMEM((near, halves, rows, shard), bf16),
+            pltpu.VMEM((count, near, halves, rows, shard), bf16),
+            pltpu.VMEM((count, near, halves, rows, shard), bf16),
             dma((5,)),
             dma((2, steps, halves)),
             dma((2, steps)),
             dma((2, 3, 2, 2)),
             dma((2, halves, 3)),
-            dma((2, steps)),
-            dma((2, 3)),
+            dma((count, near)),
+            dma((count, near)),
         ],
         compiler_params=pltpu.CompilerParams(
             collective_id=0, has_side_effects=True, vmem_limit_bytes=51 * 1024 * 1024

time: 84.3 us -> 82 us (0.973)
  the two profiles are of different devices: /device:TPU:8 before, /device:TPU:36 now
where the time goes in v3:
time: 82 us; the launch traced here: 81.8 us
  Pallas kernels  72.4 us (88%)
  waiting for transfers between devices  5.82 us (7%)
  starting transfers between devices  2.03 us (2%)
  local copies, waits for them, and re-layouts  1.52 us (2%)
    pallas_call x1, Pallas kernels, project(): pl.pallas_call(functools.partial(project_kernel, near), out_shape=jax.Sha...  64.5 us
    pallas_call x1, Pallas kernels, page_attention(): pl.pallas_call(functools.partial(attention_kernel, table_len // 2), out_s...  7.86 us
    ppermute x2, waiting for transfers between devices, moved(): return lax.ppermute(o_weight, 'fsdp', pairs)  5.82 us
    ppermute x2, starting transfers between devices, moved(): return lax.ppermute(o_weight, 'fsdp', pairs)  2.03 us
  transfers between devices with their start and end apart: 2, of which 2 were waited for; matrix products, arithmetic and copies ran while one was open for 0% of the time, Pallas kernels for 10%

profile of v3, /device:TPU:36, one launch (start us, length us, event | category | flops | bytes accessed | tf_op | source)
XLA Modules:
  0.0 81.8 jit_solution(4540770928492626677)
XLA Ops:
  0.0 1.9 %collective-permute-start = (bf16[1024,256]{1,0:T(8,128)(2,1)}, bf16[1024,256]{1,0:T(8,128)(2,1)S(1)}, u32[]{:S(2)}, u32[]{:S(2)}) collective-permute-start(bf16[1024,256]{1,0:T(8,128)(2,1)} %weight_hbm.1), channel_id=1, source_target_pairs={{0,4},{1,5},{2,6},{3,7},{4,8},{5,9},{6,10},{7,11},{8,12},{9,13},{1... | collective-permute-start | bytes 1572872 | tf_op jit(solution)/shard_map/ppermute | solution.py:661
  1.9 0.1 collective-permute-start.1
  2.0 0.0 copy-start
  2.0 7.9 %shard_map.91 = (bf16[8,2,3,128,128]{4,3,2,1,0:T(8,128)(2,1)}, f32[8,8,128]{2,1,0:T(8,128)}) custom-call(s32[16,24]{1,0:T(8,128)} %bitcast.6, s32[24]{0:T(128)} %lengths_ref.1, s32[4,24]{1,0:T(4,128)} %bitcast.7, bf16[24,4,8192]{2,1,0:T(4,128)(2,1)} %query_hbm.1, bf16[24,64,1024]{2,1,0:T(8,128)(2,1)} %keys_hbm.1, bf16[24,64,1024]{2,1,0:T(8,128)(2,1)} %values_hbm.1, ...), custom_call_target="tpu_custom_call" | custom-call | flops 10000000000 | bytes 10000000 | tf_op jit(solution)/shard_map/pallas_call | solution.py:298
  9.9 4.0 %collective-permute-done.weight_below = bf16[1024,256]{1,0:T(8,128)(2,1)S(1)} collective-permute-done((bf16[1024,256]{1,0:T(8,128)(2,1)}, bf16[1024,256]{1,0:T(8,128)(2,1)S(1)}, u32[]{:S(2)}, u32[]{:S(2)}) %collective-permute-start) | collective-permute-done | bytes 524320 | tf_op jit(solution)/shard_map/ppermute | solution.py:661
  13.9 1.8 %collective-permute-done.1.weight_above = bf16[1024,256]{1,0:T(8,128)(2,1)S(1)} collective-permute-done((bf16[1024,256]{1,0:T(8,128)(2,1)}, bf16[1024,256]{1,0:T(8,128)(2,1)S(1)}, u32[]{:S(2)}, u32[]{:S(2)}) %collective-permute-start.1) | collective-permute-done | bytes 524320 | tf_op jit(solution)/shard_map/ppermute | solution.py:661
  15.7 0.0 copy-done
  15.7 0.0 copy-start.1
  15.7 0.8 copy-done.1
  16.5 64.5 %shard_map.92 = bf16[96,1024]{1,0:T(8,128)(2,1)S(1)} custom-call(bf16[8,2,3,128,128]{4,3,2,1,0:T(8,128)(2,1)} %get-tuple-element.7.part_hbm, f32[8,8,128]{2,1,0:T(8,128)S(1)} %copy-done.1, bf16[1024,256]{1,0:T(8,128)(2,1)S(1)} %copy-done, bf16[1024,256]{1,0:T(8,128)(2,1)S(1)} %collective-permute-done.weight_below, ...), custom_call_target="tpu_custom_call" | custom-call | tf_op jit(solution)/shard_map/pallas_call | solution.py:622
  81.0 0.8 reshape.11
Async XLA Ops:
  0.0 13.9 %collective-permute-start = (bf16[1024,256]{1,0:T(8,128)(2,1)}, bf16[1024,256]{1,0:T(8,128)(2,1)S(1)}, u32[]{:S(2)}, u32[]{:S(2)}) collective-permute-start(bf16[1024,256]{1,0:T(8,128)(2,1)} %weight_hbm.1), channel_id=1, source_target_pairs={{0,4},{1,5},{2,6},{3,7},{4,8},{5,9},{6,10},{7,11},{8,12},{9,13},{1... | collective-permute-start | bytes 1572872 | tf_op jit(solution)/shard_map/ppermute | solution.py:661
  1.9 13.8 %collective-permute-start.1 = (bf16[1024,256]{1,0:T(8,128)(2,1)}, bf16[1024,256]{1,0:T(8,128)(2,1)S(1)}, u32[]{:S(2)}, u32[]{:S(2)}) collective-permute-start(bf16[1024,256]{1,0:T(8,128)(2,1)} %weight_hbm.1), channel_id=1, source_target_pairs={{0,28},{1,29},{2,30},{3,31},{4,0},{5,1},{6,2},{7,3},{8,4},{9,5},{1... | collective-permute-start | bytes 1572872 | tf_op jit(solution)/shard_map/ppermute | solution.py:661
  2.0 13.7 %copy-start = (bf16[1024,256]{1,0:T(8,128)(2,1)S(1)}, bf16[1024,256]{1,0:T(8,128)(2,1)}, u32[]{:S(2)}) copy-start(bf16[1024,256]{1,0:T(8,128)(2,1)} %weight_hbm.1) | copy-start | bytes 1572868
  15.7 0.8 copy-start.1

commit v4 on v2

--- a/solution.py
+++ b/solution.py
@@ -142,14 +142,16 @@
             [part[: rows // 2] for part in parts] + [part[rows // 2 :] for part in parts], axis=0
         )
 
-    def block(keys, values, query, live):
+    def score(keys, query, live):
         scores = (
             lax.dot_general(
                 keys, query, (((1,), (1,)), ((), ())), preferred_element_type=jnp.float32
             )
             * scale
         )
-        scores = jnp.where(live, scores, DEAD)
+        return jnp.where(live, scores, DEAD)
+
+    def weigh(scores, values):
         block_max = jnp.max(scores, axis=0, keepdims=True)
         expo = jnp.exp2(scores - jnp.maximum(block_max, 0.1 * DEAD))
         block_sum = jnp.sum(expo, axis=0, keepdims=True)
@@ -160,6 +162,9 @@
             preferred_element_type=jnp.float32,
         )
         return block_max, block_sum, block_out
+
+    def block(keys, values, query, live):
+        return weigh(score(keys, query, live), values)
 
     def new_block(group):
         bits = jnp.zeros((1, lanes), jnp.int32)
@@ -199,14 +204,18 @@
         run_sum = sum_ref[...]
         next_max = []
         next_sum = []
+        def kv_scores(kv):
+            return score(
+                keys_ref[slot, :, kv * head_size : (kv + 1) * head_size], group_ref[kv], live
+            )
+
+        scores = kv_scores(0)
         for kv in range(kv_count):
             columns = slice(kv * head_size, (kv + 1) * head_size)
-            block_max, block_sum, block_out = block(
-                keys_ref[slot, :, columns],
-                values_ref[slot, :, columns],
-                group_ref[kv],
-                live,
-            )
+            ready = scores
+            if kv + 1 < kv_count:
+                scores = kv_scores(kv + 1)
+            block_max, block_sum, block_out = weigh(ready, values_ref[slot, :, columns])
             old_max = run_max[kv : kv + 1]
             new_max = jnp.maximum(old_max, block_max)
             keep = jnp.exp2(old_max - new_max)
@@ -370,7 +379,8 @@
     lse_sems,
     ring_sems,
     gather_sems,
-    shard_sems,
+    shard_send,
+    shard_recv,
     final_sems,
 ):
     count = lax.axis_size("ctx")
@@ -538,35 +548,68 @@
             gathers[half, index].wait_recv()
     for copy in own_copies[2:]:
         copy.wait()
-    receive(4, 0)
-    receive(4, 1)
-
+
+    order = [dx * 2 + dy for dx, dy in (*CTX_STEPS, (0, 0))]
+    far = (z + count // 2) % count
+    far_step = (far // 2 - c // 2 + count // 2) % (count // 2) * 2 + (far % 2 + c % 2) % 2
     shard_copies = []
 
-    def project(column):
+    def project(turn):
+        step = order[turn]
+        for early in range(3):
+            late = early + 3
+            if turn == early:
+                step = jnp.where(far_step == order[early], order[late], order[early])
+            if turn == late:
+                step = jnp.where(far_step == order[early], order[early], order[late])
+        column = ctx_step(step // 2, step % 2)
         for half in range(halves):
             value = gathered[half].reshape(near * rows, weights.shape[1])
             result = jnp.dot(value, weights[column], preferred_element_type=jnp.float32)
             product[column, half * near * rows : (half + 1) * near * rows] = result.astype(
                 jnp.bfloat16
             )
-
-    for index, other in enumerate(others):
-        project(other)
-        shard_copies.append(
-            send(product.at[other], shard_in.at[index], shard_sems, (index,), at_ctx(other))
-        )
-    project(c)
-    for copy in shard_copies:
-        copy.wait_recv()
+        copy = pltpu.make_async_remote_copy(
+            src_ref=product.at[column],
+            dst_ref=shard_in.at[c],
+            send_sem=shard_send.at[turn],
+            recv_sem=shard_recv.at[c],
+            device_id=at_ctx(column),
+            device_id_type=MESH,
+        )
+        shard_copies.append((copy, column))
+
+        @pl.when(column != c)
+        def _():
+            copy.start()
+
+    for turn in range(count):
+        if turn == 3:
+            receive(4, 0)
+            receive(4, 1)
+        project(turn)
+    shard_in[c] = product[c]
+    for other in range(count):
+
+        @pl.when(other != c)
+        def _():
+            pltpu.make_async_remote_copy(
+                src_ref=shard_in.at[other],
+                dst_ref=shard_in.at[other],
+                send_sem=shard_send.at[0],
+                recv_sem=shard_recv.at[other],
+                device_id=at_z(1),
+                device_id_type=MESH,
+            ).wait_recv()
+
     final_copies = []
     for index, owner in enumerate([*locals_[::-1], r]):
         for half in range(halves):
             base = pl.multiple_of((half * near + owner) * rows, rows)
             span = pl.ds(base, rows)
-            value = product[c, span].astype(jnp.float32)
-            for step in range(steps):
-                value = value + shard_in[step, span].astype(jnp.float32)
+            value = shard_in[0, span].astype(jnp.float32)
+            for other in range(1, count):
+                value = value + shard_in[other, span].astype(jnp.float32)
             summed[owner, half] = value.astype(jnp.bfloat16)
         if index < near - 1:
             final_copies.append(
@@ -582,7 +625,13 @@
                 out_ref[start : start + token_rows, source * shard : (source + 1) * shard] = final[
                     source, half, group * token_rows : (group + 1) * token_rows
                 ]
-    started = lse_copies + part_copies[1] + shard_copies + final_copies
+    for copy, column in shard_copies:
+
+        @pl.when(column != c)
+        def _():
+            copy.wait_send()
+
+    started = lse_copies + part_copies[1] + final_copies
     for copies in (ring, gathers):
         started += copies.values()
     for copy in started:
@@ -611,7 +660,7 @@
             pltpu.VMEM((groups, head_size, lanes), f32),
             pltpu.VMEM((halves, near, rows, width), bf16),
             pltpu.VMEM((count, near * halves * rows, shard), bf16),
-            pltpu.VMEM((steps, near * halves * rows, shard), bf16),
+            pltpu.VMEM((count, near * halves * rows, shard), bf16),
             pltpu.VMEM((near, halves, rows, shard), bf16),
             pltpu.VMEM((near, halves, rows, shard), bf16),
             dma((5,)),
@@ -619,7 +668,8 @@
             dma((2, steps)),
             dma((2, 3, 2, 2)),
             dma((2, halves, 3)),
-            dma((2, steps)),
+            dma((count,)),
+            dma((count,)),
             dma((2, 3)),
         ],
         compiler_params=pltpu.CompilerParams(

time: 84.3 us -> 79 us (0.937)
  the two profiles are of different devices: /device:TPU:8 before, /device:TPU:12 now
where the time goes in v4:
time: 79 us; the launch traced here: 78.6 us
  Pallas kernels  66.7 us (84%)
  starting transfers between devices  5.86 us (7%)
  waiting for transfers between devices  4.52 us (6%)
  local copies, waits for them, and re-layouts  1.52 us (2%)
    pallas_call x1, Pallas kernels, project(): pl.pallas_call(functools.partial(project_kernel, near), out_shape=jax.Sha...  59.1 us
    pallas_call x1, Pallas kernels, page_attention(): pl.pallas_call(functools.partial(attention_kernel, table_len // 2), out_s...  7.6 us
    ppermute x2, starting transfers between devices, moved(): return lax.ppermute(o_weight, 'fsdp', pairs)  5.86 us
    ppermute x2, waiting for transfers between devices, moved(): return lax.ppermute(o_weight, 'fsdp', pairs)  4.52 us
  transfers between devices with their start and end apart: 2, of which 1 were waited for; matrix products, arithmetic and copies ran while one was open for 0% of the time, Pallas kernels for 10%

profile of v4, /device:TPU:12, one launch (start us, length us, event | category | flops | bytes accessed | tf_op | source)
XLA Modules:
  0.0 78.6 jit_solution(516979814391542612)
XLA Ops:
  0.0 1.9 %collective-permute-start = (bf16[1024,256]{1,0:T(8,128)(2,1)}, bf16[1024,256]{1,0:T(8,128)(2,1)S(1)}, u32[]{:S(2)}, u32[]{:S(2)}) collective-permute-start(bf16[1024,256]{1,0:T(8,128)(2,1)} %weight_hbm.1), channel_id=1, source_target_pairs={{0,4},{1,5},{2,6},{3,7},{4,8},{5,9},{6,10},{7,11},{8,12},{9,13},{1... | collective-permute-start | bytes 1572872 | tf_op jit(solution)/shard_map/ppermute | solution.py:691
  1.9 3.9 %collective-permute-start.1 = (bf16[1024,256]{1,0:T(8,128)(2,1)}, bf16[1024,256]{1,0:T(8,128)(2,1)S(1)}, u32[]{:S(2)}, u32[]{:S(2)}) collective-permute-start(bf16[1024,256]{1,0:T(8,128)(2,1)} %weight_hbm.1), channel_id=1, source_target_pairs={{0,28},{1,29},{2,30},{3,31},{4,0},{5,1},{6,2},{7,3},{8,4},{9,5},{1... | collective-permute-start | bytes 1572872 | tf_op jit(solution)/shard_map/ppermute | solution.py:691
  5.9 0.0 copy-start
  5.9 7.6 %shard_map.91 = (bf16[8,2,3,128,128]{4,3,2,1,0:T(8,128)(2,1)}, f32[8,8,128]{2,1,0:T(8,128)}) custom-call(s32[16,24]{1,0:T(8,128)} %bitcast.6, s32[24]{0:T(128)} %lengths_ref.1, s32[4,24]{1,0:T(4,128)} %bitcast.7, bf16[24,4,8192]{2,1,0:T(4,128)(2,1)} %query_hbm.1, bf16[24,64,1024]{2,1,0:T(8,128)(2,1)} %keys_hbm.1, bf16[24,64,1024]{2,1,0:T(8,128)(2,1)} %values_hbm.1, ...), custom_call_target="tpu_custom_call" | custom-call | flops 10000000000 | bytes 10000000 | tf_op jit(solution)/shard_map/pallas_call | solution.py:307
  13.5 4.5 %collective-permute-done.weight_below = bf16[1024,256]{1,0:T(8,128)(2,1)S(1)} collective-permute-done((bf16[1024,256]{1,0:T(8,128)(2,1)}, bf16[1024,256]{1,0:T(8,128)(2,1)S(1)}, u32[]{:S(2)}, u32[]{:S(2)}) %collective-permute-start) | collective-permute-done | bytes 524320 | tf_op jit(solution)/shard_map/ppermute | solution.py:691
  18.0 0.0 collective-permute-done.1.weight_above
  18.0 0.0 copy-done
  18.0 0.0 copy-start.1
  18.0 0.8 copy-done.1
  18.8 59.1 %shard_map.92 = bf16[96,1024]{1,0:T(8,128)(2,1)S(1)} custom-call(bf16[8,2,3,128,128]{4,3,2,1,0:T(8,128)(2,1)} %get-tuple-element.7.part_hbm, f32[8,8,128]{2,1,0:T(8,128)S(1)} %copy-done.1, bf16[1024,256]{1,0:T(8,128)(2,1)S(1)} %copy-done, bf16[1024,256]{1,0:T(8,128)(2,1)S(1)} %collective-permute-done.weight_below, ...), custom_call_target="tpu_custom_call" | custom-call | tf_op jit(solution)/shard_map/pallas_call | solution.py:649
  77.8 0.8 reshape.11
Async XLA Ops:
  0.0 18.0 %collective-permute-start = (bf16[1024,256]{1,0:T(8,128)(2,1)}, bf16[1024,256]{1,0:T(8,128)(2,1)S(1)}, u32[]{:S(2)}, u32[]{:S(2)}) collective-permute-start(bf16[1024,256]{1,0:T(8,128)(2,1)} %weight_hbm.1), channel_id=1, source_target_pairs={{0,4},{1,5},{2,6},{3,7},{4,8},{5,9},{6,10},{7,11},{8,12},{9,13},{1... | collective-permute-start | bytes 1572872 | tf_op jit(solution)/shard_map/ppermute | solution.py:691
  1.9 16.1 %collective-permute-start.1 = (bf16[1024,256]{1,0:T(8,128)(2,1)}, bf16[1024,256]{1,0:T(8,128)(2,1)S(1)}, u32[]{:S(2)}, u32[]{:S(2)}) collective-permute-start(bf16[1024,256]{1,0:T(8,128)(2,1)} %weight_hbm.1), channel_id=1, source_target_pairs={{0,28},{1,29},{2,30},{3,31},{4,0},{5,1},{6,2},{7,3},{8,4},{9,5},{1... | collective-permute-start | bytes 1572872 | tf_op jit(solution)/shard_map/ppermute | solution.py:691
  5.9 12.1 %copy-start = (bf16[1024,256]{1,0:T(8,128)(2,1)S(1)}, bf16[1024,256]{1,0:T(8,128)(2,1)}, u32[]{:S(2)}) copy-start(bf16[1024,256]{1,0:T(8,128)(2,1)} %weight_hbm.1) | copy-start | bytes 1572868
  18.0 0.8 copy-start.1

commit v5 on v4

--- a/solution.py
+++ b/solution.py
@@ -10,6 +10,8 @@
 SHARE = 8
 DEAD = -1e30
 LOG2E = 1.4426950408889634
+LSE_ROWS = 8
+LSE_ROOM = 1024
 
 
 def attention_kernel(
@@ -23,7 +25,7 @@
     new_keys_hbm,
     new_values_hbm,
     out_hbm,
-    lse_ref,
+    lse_hbm,
     query_ref,
     group_ref,
     new_keys_ref,
@@ -32,12 +34,14 @@
     max_ref,
     sum_ref,
     out_ref,
+    lse_ref,
     keys_ref,
     values_ref,
     unit_ref,
     query_sem,
     new_sem,
     out_sem,
+    lse_sem,
     key_sem,
     value_sem,
 ):
@@ -246,6 +250,7 @@
                 :, half * (lanes // 2) : (half + 1) * (lanes // 2)
             ]
 
+    lse_ref[...] = jnp.zeros(lse_ref.shape, jnp.float32)
     out_copies = []
     for group in range(groups):
         query_copies[group].wait()
@@ -284,6 +289,9 @@
         copy = pltpu.make_async_copy(out_ref.at[group], out_hbm.at[:, :, group], out_sem.at[group])
         copy.start()
         out_copies.append(copy)
+    copy = pltpu.make_async_copy(lse_ref, lse_hbm.at[:, pl.ds(0, lse_ref.shape[1])], lse_sem)
+    copy.start()
+    out_copies.append(copy)
     for copy in out_copies:
         copy.wait()
 
@@ -308,10 +316,10 @@
         functools.partial(attention_kernel, table_len // 2),
         out_shape=(
             jax.ShapeDtypeStruct((kv_count, 2, groups, head_size, lanes // 2), bf16),
-            jax.ShapeDtypeStruct((kv_count, 8, lanes // 2), f32),
+            jax.ShapeDtypeStruct((kv_count, LSE_ROOM, lanes // 2), f32),
         ),
         in_specs=[smem, smem, smem] + [anywhere] * 5,
-        out_specs=(anywhere, vmem),
+        out_specs=(anywhere, anywhere),
         scratch_shapes=[
             pltpu.VMEM(query.shape, bf16),
             pltpu.VMEM((kv_count, lanes, head_size), bf16),
@@ -321,12 +329,14 @@
             pltpu.VMEM((kv_count, lanes), f32),
             pltpu.VMEM((kv_count, lanes), f32),
             pltpu.VMEM((groups, kv_count, 2, head_size, lanes // 2), bf16),
+            pltpu.VMEM((kv_count, LSE_ROWS, lanes // 2), f32),
             pltpu.VMEM((slots, page_len, width), bf16),
             pltpu.VMEM((slots, page_len, width), bf16),
             pltpu.SMEM((3, units), jnp.int32),
             dma((groups,)),
             dma((2,)),
             dma((groups,)),
+            dma,
             dma((slots,)),
             dma((slots,)),
         ],
@@ -372,6 +382,7 @@
     gathered,
     product,
     shard_in,
+    sums,
     summed,
     final,
     own_sems,
@@ -422,7 +433,7 @@
         pltpu.make_async_copy(source, target, own_sems.at[index])
         for index, (source, target) in enumerate(
             (
-                (lse_hbm.at[c], lse_own),
+                (lse_hbm.at[c, pl.ds(0, LSE_ROWS)], lse_own),
                 (part_hbm.at[c], part_own),
                 (weight_hbm, weights.at[z]),
                 (weight_below, weights.at[below]),
@@ -447,7 +458,13 @@
         return copy
 
     lse_copies = [
-        send(lse_hbm.at[other], lse_in.at[index], lse_sems, (index,), at_ctx(other))
+        send(
+            lse_hbm.at[other, pl.ds(0, LSE_ROWS)],
+            lse_in.at[index],
+            lse_sems,
+            (index,),
+            at_ctx(other),
+        )
         for index, other in enumerate(others)
     ]
 
@@ -588,29 +605,23 @@
             receive(4, 0)
             receive(4, 1)
         project(turn)
-    shard_in[c] = product[c]
-    for other in range(count):
-
-        @pl.when(other != c)
-        def _():
-            pltpu.make_async_remote_copy(
-                src_ref=shard_in.at[other],
-                dst_ref=shard_in.at[other],
-                send_sem=shard_send.at[0],
-                recv_sem=shard_recv.at[other],
-                device_id=at_z(1),
-                device_id_type=MESH,
-            ).wait_recv()
-
+    sums[...] = product[c].astype(jnp.float32)
+    for dx, dy in CTX_STEPS:
+        other = ctx_step(count // 2 - dx, dy)
+        pltpu.make_async_remote_copy(
+            src_ref=shard_in.at[other],
+            dst_ref=shard_in.at[other],
+            send_sem=shard_send.at[0],
+            recv_sem=shard_recv.at[other],
+            device_id=at_z(1),
+            device_id_type=MESH,
+        ).wait_recv()
+        sums[...] += shard_in[other].astype(jnp.float32)
     final_copies = []
     for index, owner in enumerate([*locals_[::-1], r]):
         for half in range(halves):
-            base = pl.multiple_of((half * near + owner) * rows, rows)
-            span = pl.ds(base, rows)
-            value = shard_in[0, span].astype(jnp.float32)
-            for other in range(1, count):
-                value = value + shard_in[other, span].astype(jnp.float32)
-            summed[owner, half] = value.astype(jnp.bfloat16)
+            span = pl.ds(pl.multiple_of((half * near + owner) * rows, rows), rows)
+            summed[owner, half] = sums[span].astype(jnp.bfloat16)
         if index < near - 1:
             final_copies.append(
                 send(summed.at[owner], final.at[r], final_sems, (index,), at_local(owner))
@@ -655,12 +666,13 @@
             pltpu.VMEM((count,) + weight.shape, bf16),
             pltpu.VMEM((halves, groups, head_size, lanes), bf16),
             pltpu.VMEM((steps, halves, groups, head_size, lanes), bf16),
-            pltpu.VMEM(lse.shape[1:], f32),
-            pltpu.VMEM((steps,) + lse.shape[1:], f32),
+            pltpu.VMEM((LSE_ROWS, lanes), f32),
+            pltpu.VMEM((steps, LSE_ROWS, lanes), f32),
             pltpu.VMEM((groups, head_size, lanes), f32),
             pltpu.VMEM((halves, near, rows, width), bf16),
             pltpu.VMEM((count, near * halves * rows, shard), bf16),
             pltpu.VMEM((count, near * halves * rows, shard), bf16),
+            pltpu.VMEM((near * halves * rows, shard), f32),
             pltpu.VMEM((near, halves, rows, shard), bf16),
             pltpu.VMEM((near, halves, rows, shard), bf16),
             dma((5,)),

time: 79 us -> 78.4 us (level)
  waiting for transfers between devices: 4.52 us -> 6.59 us
  Pallas kernels: 66.7 us -> 65 us
    ppermute x2, waiting for transfers between devices: 4.52 us -> 6.59 us  [moved(): return lax.ppermute(o_weight, 'fsdp', pairs)]
    pallas_call x1, Pallas kernels: 7.6 us -> 5.53 us  [page_attention(): pl.pallas_call(functools.partial(attention_kernel, table_len // 2), out_s...]
  transfers between devices with their start and end apart: 2 -> 2, of which waited for: 1 -> 1; matrix products, arithmetic and copies ran while one was open for 0% -> 0% of each run, Pallas kernels for 10% -> 7%
where the time goes in v5:
time: 78.4 us; the launch traced here: 78.2 us
  Pallas kernels  65 us (83%)
  waiting for transfers between devices  6.59 us (8%)
  starting transfers between devices  5.86 us (7%)
    pallas_call x1, Pallas kernels, project(): pl.pallas_call(functools.partial(project_kernel, near), out_shape=jax.Sha...  59.5 us
    ppermute x2, waiting for transfers between devices, moved(): return lax.ppermute(o_weight, 'fsdp', pairs)  6.59 us
    ppermute x2, starting transfers between devices, moved(): return lax.ppermute(o_weight, 'fsdp', pairs)  5.86 us
    pallas_call x1, Pallas kernels, page_attention(): pl.pallas_call(functools.partial(attention_kernel, table_len // 2), out_s...  5.53 us
  transfers between devices with their start and end apart: 2, of which 1 were waited for; matrix products, arithmetic and copies ran while one was open for 0% of the time, Pallas kernels for 7%

profile of v5, /device:TPU:12, one launch (start us, length us, event | category | flops | bytes accessed | tf_op | source)
XLA Modules:
  0.0 78.2 jit_solution(6437539383324806504)
XLA Ops:
  0.0 1.9 %collective-permute-start = (bf16[1024,256]{1,0:T(8,128)(2,1)}, bf16[1024,256]{1,0:T(8,128)(2,1)S(1)}, u32[]{:S(2)}, u32[]{:S(2)}) collective-permute-start(bf16[1024,256]{1,0:T(8,128)(2,1)} %weight_hbm.1), channel_id=1, source_target_pairs={{0,4},{1,5},{2,6},{3,7},{4,8},{5,9},{6,10},{7,11},{8,12},{9,13},{1... | collective-permute-start | bytes 1572872 | tf_op jit(solution)/shard_map/ppermute | solution.py:703
  1.9 3.9 %collective-permute-start.1 = (bf16[1024,256]{1,0:T(8,128)(2,1)}, bf16[1024,256]{1,0:T(8,128)(2,1)S(1)}, u32[]{:S(2)}, u32[]{:S(2)}) collective-permute-start(bf16[1024,256]{1,0:T(8,128)(2,1)} %weight_hbm.1), channel_id=1, source_target_pairs={{0,28},{1,29},{2,30},{3,31},{4,0},{5,1},{6,2},{7,3},{8,4},{9,5},{1... | collective-permute-start | bytes 1572872 | tf_op jit(solution)/shard_map/ppermute | solution.py:703
  5.9 0.0 copy-start
  5.9 5.5 %shard_map.91 = (bf16[8,2,3,128,128]{4,3,2,1,0:T(8,128)(2,1)}, f32[8,1024,128]{2,1,0:T(8,128)}) custom-call(s32[16,24]{1,0:T(8,128)} %bitcast.6, s32[24]{0:T(128)} %lengths_ref.1, s32[4,24]{1,0:T(4,128)} %bitcast.7, bf16[24,4,8192]{2,1,0:T(4,128)(2,1)} %query_hbm.1, bf16[24,64,1024]{2,1,0:T(8,128)(2,1)} %keys_hbm.1, bf16[24,64,1024]{2,1,0:T(8,128)(2,1)} %values_hbm.1, ...), custom_call_target="tpu_custom_call" | custom-call | flops 10000000000 | bytes 10000000 | tf_op jit(solution)/shard_map/pallas_call | solution.py:315
  11.4 6.6 %collective-permute-done.weight_below = bf16[1024,256]{1,0:T(8,128)(2,1)S(1)} collective-permute-done((bf16[1024,256]{1,0:T(8,128)(2,1)}, bf16[1024,256]{1,0:T(8,128)(2,1)S(1)}, u32[]{:S(2)}, u32[]{:S(2)}) %collective-permute-start) | collective-permute-done | bytes 524320 | tf_op jit(solution)/shard_map/ppermute | solution.py:703
  18.0 0.0 collective-permute-done.1.weight_above
  18.0 0.0 copy-done
  18.0 59.5 %shard_map.92 = bf16[96,1024]{1,0:T(8,128)(2,1)S(1)} custom-call(bf16[8,2,3,128,128]{4,3,2,1,0:T(8,128)(2,1)} %get-tuple-element.7.part_hbm, f32[8,1024,128]{2,1,0:T(8,128)} %get-tuple-element.8.lse_hbm, bf16[1024,256]{1,0:T(8,128)(2,1)S(1)} %copy-done, bf16[1024,256]{1,0:T(8,128)(2,1)S(1)} %collective-permute-done.weight_below, ...), custom_call_target="tpu_custom_call" | custom-call | tf_op jit(solution)/shard_map/pallas_call | solution.py:660
  77.5 0.8 reshape.11
Async XLA Ops:
  0.0 18.0 %collective-permute-start = (bf16[1024,256]{1,0:T(8,128)(2,1)}, bf16[1024,256]{1,0:T(8,128)(2,1)S(1)}, u32[]{:S(2)}, u32[]{:S(2)}) collective-permute-start(bf16[1024,256]{1,0:T(8,128)(2,1)} %weight_hbm.1), channel_id=1, source_target_pairs={{0,4},{1,5},{2,6},{3,7},{4,8},{5,9},{6,10},{7,11},{8,12},{9,13},{1... | collective-permute-start | bytes 1572872 | tf_op jit(solution)/shard_map/ppermute | solution.py:703
  1.9 16.1 %collective-permute-start.1 = (bf16[1024,256]{1,0:T(8,128)(2,1)}, bf16[1024,256]{1,0:T(8,128)(2,1)S(1)}, u32[]{:S(2)}, u32[]{:S(2)}) collective-permute-start(bf16[1024,256]{1,0:T(8,128)(2,1)} %weight_hbm.1), channel_id=1, source_target_pairs={{0,28},{1,29},{2,30},{3,31},{4,0},{5,1},{6,2},{7,3},{8,4},{9,5},{1... | collective-permute-start | bytes 1572872 | tf_op jit(solution)/shard_map/ppermute | solution.py:703
  5.9 12.1 %copy-start = (bf16[1024,256]{1,0:T(8,128)(2,1)S(1)}, bf16[1024,256]{1,0:T(8,128)(2,1)}, u32[]{:S(2)}) copy-start(bf16[1024,256]{1,0:T(8,128)(2,1)} %weight_hbm.1) | copy-start | bytes 1572868

commit v6 on v5

--- a/solution.py
+++ b/solution.py
@@ -553,10 +553,10 @@
         gathers[half, 2] = send(block, block, gather_sems, (half, 2), at_local(locals_[0]))
 
     receive(2, 0)
+    receive(2, 1)
     combine(0)
-    receive(2, 1)
+    receive(3, 0)
     relay(0)
-    receive(3, 0)
     combine(1)
     relay(1)
     receive(3, 1)

time: 78.4 us -> 79.1 us (level)
  waiting for transfers between devices: 6.59 us -> 7.9 us
  Pallas kernels: 65 us -> 63.7 us
    ppermute x2, waiting for transfers between devices: 6.59 us -> 7.9 us  [moved(): return lax.ppermute(o_weight, 'fsdp', pairs)]
    pallas_call x1, Pallas kernels: 5.53 us -> 4.22 us  [page_attention(): pl.pallas_call(functools.partial(attention_kernel, table_len // 2), out_s...]
  transfers between devices with their start and end apart: 2 -> 2, of which waited for: 1 -> 1; matrix products, arithmetic and copies ran while one was open for 0% -> 0% of each run, Pallas kernels for 7% -> 5%
where the time goes in v6:
time: 79.1 us; the launch traced here: 78.2 us
  Pallas kernels  63.7 us (81%)
  waiting for transfers between devices  7.9 us (10%)
  starting transfers between devices  5.86 us (7%)
    pallas_call x1, Pallas kernels, project(): pl.pallas_call(functools.partial(project_kernel, near), out_shape=jax.Sha...  59.5 us
    ppermute x2, waiting for transfers between devices, moved(): return lax.ppermute(o_weight, 'fsdp', pairs)  7.9 us
    ppermute x2, starting transfers between devices, moved(): return lax.ppermute(o_weight, 'fsdp', pairs)  5.86 us
    pallas_call x1, Pallas kernels, page_attention(): pl.pallas_call(functools.partial(attention_kernel, table_len // 2), out_s...  4.22 us
  transfers between devices with their start and end apart: 2, of which 1 were waited for; matrix products, arithmetic and copies ran while one was open for 0% of the time, Pallas kernels for 5%

profile of v6, /device:TPU:12, one launch (start us, length us, event | category | flops | bytes accessed | tf_op | source)
XLA Modules:
  0.0 78.2 jit_solution(6883123187179658021)
XLA Ops:
  0.0 1.9 %collective-permute-start = (bf16[1024,256]{1,0:T(8,128)(2,1)}, bf16[1024,256]{1,0:T(8,128)(2,1)S(1)}, u32[]{:S(2)}, u32[]{:S(2)}) collective-permute-start(bf16[1024,256]{1,0:T(8,128)(2,1)} %weight_hbm.1), channel_id=1, source_target_pairs={{0,4},{1,5},{2,6},{3,7},{4,8},{5,9},{6,10},{7,11},{8,12},{9,13},{1... | collective-permute-start | bytes 1572872 | tf_op jit(solution)/shard_map/ppermute | solution.py:703
  1.9 3.9 %collective-permute-start.1 = (bf16[1024,256]{1,0:T(8,128)(2,1)}, bf16[1024,256]{1,0:T(8,128)(2,1)S(1)}, u32[]{:S(2)}, u32[]{:S(2)}) collective-permute-start(bf16[1024,256]{1,0:T(8,128)(2,1)} %weight_hbm.1), channel_id=1, source_target_pairs={{0,28},{1,29},{2,30},{3,31},{4,0},{5,1},{6,2},{7,3},{8,4},{9,5},{1... | collective-permute-start | bytes 1572872 | tf_op jit(solution)/shard_map/ppermute | solution.py:703
  5.9 0.0 copy-start
  5.9 4.2 %shard_map.91 = (bf16[8,2,3,128,128]{4,3,2,1,0:T(8,128)(2,1)}, f32[8,1024,128]{2,1,0:T(8,128)}) custom-call(s32[16,24]{1,0:T(8,128)} %bitcast.6, s32[24]{0:T(128)} %lengths_ref.1, s32[4,24]{1,0:T(4,128)} %bitcast.7, bf16[24,4,8192]{2,1,0:T(4,128)(2,1)} %query_hbm.1, bf16[24,64,1024]{2,1,0:T(8,128)(2,1)} %keys_hbm.1, bf16[24,64,1024]{2,1,0:T(8,128)(2,1)} %values_hbm.1, ...), custom_call_target="tpu_custom_call" | custom-call | flops 10000000000 | bytes 10000000 | tf_op jit(solution)/shard_map/pallas_call | solution.py:315
  10.1 7.9 %collective-permute-done.weight_below = bf16[1024,256]{1,0:T(8,128)(2,1)S(1)} collective-permute-done((bf16[1024,256]{1,0:T(8,128)(2,1)}, bf16[1024,256]{1,0:T(8,128)(2,1)S(1)}, u32[]{:S(2)}, u32[]{:S(2)}) %collective-permute-start) | collective-permute-done | bytes 524320 | tf_op jit(solution)/shard_map/ppermute | solution.py:703
  18.0 0.0 collective-permute-done.1.weight_above
  18.0 0.0 copy-done
  18.0 59.5 %shard_map.92 = bf16[96,1024]{1,0:T(8,128)(2,1)S(1)} custom-call(bf16[8,2,3,128,128]{4,3,2,1,0:T(8,128)(2,1)} %get-tuple-element.7.part_hbm, f32[8,1024,128]{2,1,0:T(8,128)} %get-tuple-element.8.lse_hbm, bf16[1024,256]{1,0:T(8,128)(2,1)S(1)} %copy-done, bf16[1024,256]{1,0:T(8,128)(2,1)S(1)} %collective-permute-done.weight_below, ...), custom_call_target="tpu_custom_call" | custom-call | tf_op jit(solution)/shard_map/pallas_call | solution.py:660
  77.5 0.8 reshape.11
Async XLA Ops:
  0.0 18.0 %collective-permute-start = (bf16[1024,256]{1,0:T(8,128)(2,1)}, bf16[1024,256]{1,0:T(8,128)(2,1)S(1)}, u32[]{:S(2)}, u32[]{:S(2)}) collective-permute-start(bf16[1024,256]{1,0:T(8,128)(2,1)} %weight_hbm.1), channel_id=1, source_target_pairs={{0,4},{1,5},{2,6},{3,7},{4,8},{5,9},{6,10},{7,11},{8,12},{9,13},{1... | collective-permute-start | bytes 1572872 | tf_op jit(solution)/shard_map/ppermute | solution.py:703
  1.9 16.1 %collective-permute-start.1 = (bf16[1024,256]{1,0:T(8,128)(2,1)}, bf16[1024,256]{1,0:T(8,128)(2,1)S(1)}, u32[]{:S(2)}, u32[]{:S(2)}) collective-permute-start(bf16[1024,256]{1,0:T(8,128)(2,1)} %weight_hbm.1), channel_id=1, source_target_pairs={{0,28},{1,29},{2,30},{3,31},{4,0},{5,1},{6,2},{7,3},{8,4},{9,5},{1... | collective-permute-start | bytes 1572872 | tf_op jit(solution)/shard_map/ppermute | solution.py:703
  5.9 12.1 %copy-start = (bf16[1024,256]{1,0:T(8,128)(2,1)S(1)}, bf16[1024,256]{1,0:T(8,128)(2,1)}, u32[]{:S(2)}) copy-start(bf16[1024,256]{1,0:T(8,128)(2,1)} %weight_hbm.1) | copy-start | bytes 1572868

commit v7 on v6

--- a/solution.py
+++ b/solution.py
@@ -632,10 +632,13 @@
     for source in range(near):
         for half in range(halves):
             for group in range(groups):
-                start = (group * halves + half) * token_rows
-                out_ref[start : start + token_rows, source * shard : (source + 1) * shard] = final[
-                    source, half, group * token_rows : (group + 1) * token_rows
-                ]
+                new = out_ref.shape[1]
+                size = token_rows // new
+                start = (group * halves + half) * size
+                value = final[source, half, group * token_rows : (group + 1) * token_rows]
+                out_ref[start : start + size, :, source * shard : (source + 1) * shard] = (
+                    value.reshape(size, new, shard)
+                )
     for copy, column in shard_copies:
 
         @pl.when(column != c)
@@ -649,7 +652,7 @@
         copy.wait_send()
 
 
-def project(part, lse, weight, weight_below, weight_above, near):
+def project(part, lse, weight, weight_below, weight_above, near, new):
     count, halves, groups, head_size, lanes = part.shape
     width, shard = weight.shape
     rows = groups * lanes * head_size // width
@@ -659,7 +662,7 @@
     bf16, f32, dma = jnp.bfloat16, jnp.float32, pltpu.SemaphoreType.DMA
     return pl.pallas_call(
         functools.partial(project_kernel, near),
-        out_shape=jax.ShapeDtypeStruct((halves * rows, near * shard), bf16),
+        out_shape=jax.ShapeDtypeStruct((halves * rows // new, new, near * shard), bf16),
         in_specs=[anywhere, anywhere, anywhere, vmem, vmem],
         out_specs=vmem,
         scratch_shapes=[
@@ -695,7 +698,7 @@
 ):
     ctx_count = lax.axis_size("ctx")
     fsdp_count = lax.axis_size("fsdp")
-    traj, new, _ = queries.shape
+    new = queries.shape[1]
     near = fsdp_count // ctx_count
 
     def moved(step):
@@ -706,8 +709,7 @@
     part, lse = attend(
         queries, key_pages, value_pages, new_keys, new_values, page_table, lengths, parents
     )
-    mixed = project(part, lse, o_weight, weight_below, weight_above, near)
-    return mixed.reshape(traj, new, -1)
+    return project(part, lse, o_weight, weight_below, weight_above, near, new)
 
 
 def solution(mesh):

time: 79.1 us -> 78.2 us (0.989)
  transfers between devices with their start and end apart: 2 -> 2, of which waited for: 1 -> 1; matrix products, arithmetic and copies ran while one was open for 0% -> 0% of each run, Pallas kernels for 5% -> 6%
where the time goes in v7:
time: 78.2 us; the launch traced here: 78 us
  Pallas kernels  64.2 us (82%)
  waiting for transfers between devices  7.21 us (9%)
  starting transfers between devices  5.86 us (7%)
    pallas_call x1, Pallas kernels, project(): pl.pallas_call(functools.partial(project_kernel, near), out_shape=jax.Sha...  59.3 us
    ppermute x2, waiting for transfers between devices, moved(): return lax.ppermute(o_weight, 'fsdp', pairs)  7.21 us
    ppermute x2, starting transfers between devices, moved(): return lax.ppermute(o_weight, 'fsdp', pairs)  5.86 us
    pallas_call x1, Pallas kernels, page_attention(): pl.pallas_call(functools.partial(attention_kernel, table_len // 2), out_s...  4.91 us
  transfers between devices with their start and end apart: 2, of which 1 were waited for; matrix products, arithmetic and copies ran while one was open for 0% of the time, Pallas kernels for 6%

profile of v7, /device:TPU:12, one launch (start us, length us, event | category | flops | bytes accessed | tf_op | source)
XLA Modules:
  0.0 78.0 jit_solution(11738392528833908961)
XLA Ops:
  0.0 1.9 %collective-permute-start = (bf16[1024,256]{1,0:T(8,128)(2,1)}, bf16[1024,256]{1,0:T(8,128)(2,1)S(1)}, u32[]{:S(2)}, u32[]{:S(2)}) collective-permute-start(bf16[1024,256]{1,0:T(8,128)(2,1)} %weight_hbm.1), channel_id=1, source_target_pairs={{0,4},{1,5},{2,6},{3,7},{4,8},{5,9},{6,10},{7,11},{8,12},{9,13},{1... | collective-permute-start | bytes 1572872 | tf_op jit(solution)/shard_map/ppermute | solution.py:706
  1.9 3.9 %collective-permute-start.1 = (bf16[1024,256]{1,0:T(8,128)(2,1)}, bf16[1024,256]{1,0:T(8,128)(2,1)S(1)}, u32[]{:S(2)}, u32[]{:S(2)}) collective-permute-start(bf16[1024,256]{1,0:T(8,128)(2,1)} %weight_hbm.1), channel_id=1, source_target_pairs={{0,28},{1,29},{2,30},{3,31},{4,0},{5,1},{6,2},{7,3},{8,4},{9,5},{1... | collective-permute-start | bytes 1572872 | tf_op jit(solution)/shard_map/ppermute | solution.py:706
  5.9 0.0 copy-start
  5.9 4.9 %shard_map.91 = (bf16[8,2,3,128,128]{4,3,2,1,0:T(8,128)(2,1)}, f32[8,1024,128]{2,1,0:T(8,128)}) custom-call(s32[16,24]{1,0:T(8,128)} %bitcast.6, s32[24]{0:T(128)} %lengths_ref.1, s32[4,24]{1,0:T(4,128)} %bitcast.7, bf16[24,4,8192]{2,1,0:T(4,128)(2,1)} %query_hbm.1, bf16[24,64,1024]{2,1,0:T(8,128)(2,1)} %keys_hbm.1, bf16[24,64,1024]{2,1,0:T(8,128)(2,1)} %values_hbm.1, ...), custom_call_target="tpu_custom_call" | custom-call | flops 10000000000 | bytes 10000000 | tf_op jit(solution)/shard_map/pallas_call | solution.py:315
  10.8 7.2 %collective-permute-done.weight_below = bf16[1024,256]{1,0:T(8,128)(2,1)S(1)} collective-permute-done((bf16[1024,256]{1,0:T(8,128)(2,1)}, bf16[1024,256]{1,0:T(8,128)(2,1)S(1)}, u32[]{:S(2)}, u32[]{:S(2)}) %collective-permute-start) | collective-permute-done | bytes 524320 | tf_op jit(solution)/shard_map/ppermute | solution.py:706
  18.0 0.0 collective-permute-done.1.weight_above
  18.0 0.0 copy-done
  18.0 59.3 %shard_map.92 = bf16[24,4,1024]{2,1,0:T(4,128)(2,1)S(1)} custom-call(bf16[8,2,3,128,128]{4,3,2,1,0:T(8,128)(2,1)} %get-tuple-element.7.part_hbm, f32[8,1024,128]{2,1,0:T(8,128)} %get-tuple-element.8.lse_hbm, bf16[1024,256]{1,0:T(8,128)(2,1)S(1)} %copy-done, bf16[1024,256]{1,0:T(8,128)(2,1)S(1)} %collective-permute-done.weight_below, ...), custom_call_target="tpu_custom_call" | custom-call | tf_op jit(solution)/shard_map/pallas_call | solution.py:663
  77.3 0.7 copy.11
Async XLA Ops:
  0.0 18.0 %collective-permute-start = (bf16[1024,256]{1,0:T(8,128)(2,1)}, bf16[1024,256]{1,0:T(8,128)(2,1)S(1)}, u32[]{:S(2)}, u32[]{:S(2)}) collective-permute-start(bf16[1024,256]{1,0:T(8,128)(2,1)} %weight_hbm.1), channel_id=1, source_target_pairs={{0,4},{1,5},{2,6},{3,7},{4,8},{5,9},{6,10},{7,11},{8,12},{9,13},{1... | collective-permute-start | bytes 1572872 | tf_op jit(solution)/shard_map/ppermute | solution.py:706
  1.9 16.1 %collective-permute-start.1 = (bf16[1024,256]{1,0:T(8,128)(2,1)}, bf16[1024,256]{1,0:T(8,128)(2,1)S(1)}, u32[]{:S(2)}, u32[]{:S(2)}) collective-permute-start(bf16[1024,256]{1,0:T(8,128)(2,1)} %weight_hbm.1), channel_id=1, source_target_pairs={{0,28},{1,29},{2,30},{3,31},{4,0},{5,1},{6,2},{7,3},{8,4},{9,5},{1... | collective-permute-start | bytes 1572872 | tf_op jit(solution)/shard_map/ppermute | solution.py:706
  5.9 12.1 %copy-start = (bf16[1024,256]{1,0:T(8,128)(2,1)S(1)}, bf16[1024,256]{1,0:T(8,128)(2,1)}, u32[]{:S(2)}) copy-start(bf16[1024,256]{1,0:T(8,128)(2,1)} %weight_hbm.1) | copy-start | bytes 1572868

commit v8 on v7

--- a/solution.py
+++ b/solution.py
@@ -573,12 +573,11 @@
 
     def project(turn):
         step = order[turn]
-        for early in range(3):
-            late = early + 3
+        for early, late in ((0, 4), (1, 5), (2, 6), (3, 5)):
             if turn == early:
-                step = jnp.where(far_step == order[early], order[late], order[early])
+                step = jnp.where(far_step == order[early], order[late], step)
             if turn == late:
-                step = jnp.where(far_step == order[early], order[early], order[late])
+                step = jnp.where(far_step == order[early], order[early], step)
         column = ctx_step(step // 2, step % 2)
         for half in range(halves):
             value = gathered[half].reshape(near * rows, weights.shape[1])
@@ -601,7 +600,7 @@
             copy.start()
 
     for turn in range(count):
-        if turn == 3:
+        if turn == 4:
             receive(4, 0)
             receive(4, 1)
         project(turn)

time: 78.2 us -> 77.8 us (level)
  Pallas kernels: 64.2 us -> 63.1 us
  transfers between devices with their start and end apart: 2 -> 2, of which waited for: 1 -> 1; matrix products, arithmetic and copies ran while one was open for 0% -> 0% of each run, Pallas kernels for 6% -> 5%
where the time goes in v8:
time: 77.8 us; the launch traced here: 77.5 us
  Pallas kernels  63.1 us (81%)
  waiting for transfers between devices  7.9 us (10%)
  starting transfers between devices  5.86 us (8%)
    pallas_call x1, Pallas kernels, project(): pl.pallas_call(functools.partial(project_kernel, near), out_shape=jax.Sha...  58.8 us
    ppermute x2, waiting for transfers between devices, moved(): return lax.ppermute(o_weight, 'fsdp', pairs)  7.9 us
    ppermute x2, starting transfers between devices, moved(): return lax.ppermute(o_weight, 'fsdp', pairs)  5.86 us
    pallas_call x1, Pallas kernels, page_attention(): pl.pallas_call(functools.partial(attention_kernel, table_len // 2), out_s...  4.22 us
  transfers between devices with their start and end apart: 2, of which 1 were waited for; matrix products, arithmetic and copies ran while one was open for 0% of the time, Pallas kernels for 5%

profile of v8, /device:TPU:12, one launch (start us, length us, event | category | flops | bytes accessed | tf_op | source)
XLA Modules:
  0.0 77.5 jit_solution(8689375199235520767)
XLA Ops:
  0.0 1.9 %collective-permute-start = (bf16[1024,256]{1,0:T(8,128)(2,1)}, bf16[1024,256]{1,0:T(8,128)(2,1)S(1)}, u32[]{:S(2)}, u32[]{:S(2)}) collective-permute-start(bf16[1024,256]{1,0:T(8,128)(2,1)} %weight_hbm.1), channel_id=1, source_target_pairs={{0,4},{1,5},{2,6},{3,7},{4,8},{5,9},{6,10},{7,11},{8,12},{9,13},{1... | collective-permute-start | bytes 1572872 | tf_op jit(solution)/shard_map/ppermute | solution.py:705
  1.9 3.9 %collective-permute-start.1 = (bf16[1024,256]{1,0:T(8,128)(2,1)}, bf16[1024,256]{1,0:T(8,128)(2,1)S(1)}, u32[]{:S(2)}, u32[]{:S(2)}) collective-permute-start(bf16[1024,256]{1,0:T(8,128)(2,1)} %weight_hbm.1), channel_id=1, source_target_pairs={{0,28},{1,29},{2,30},{3,31},{4,0},{5,1},{6,2},{7,3},{8,4},{9,5},{1... | collective-permute-start | bytes 1572872 | tf_op jit(solution)/shard_map/ppermute | solution.py:705
  5.9 0.0 copy-start
  5.9 4.2 %shard_map.91 = (bf16[8,2,3,128,128]{4,3,2,1,0:T(8,128)(2,1)}, f32[8,1024,128]{2,1,0:T(8,128)}) custom-call(s32[16,24]{1,0:T(8,128)} %bitcast.6, s32[24]{0:T(128)} %lengths_ref.1, s32[4,24]{1,0:T(4,128)} %bitcast.7, bf16[24,4,8192]{2,1,0:T(4,128)(2,1)} %query_hbm.1, bf16[24,64,1024]{2,1,0:T(8,128)(2,1)} %keys_hbm.1, bf16[24,64,1024]{2,1,0:T(8,128)(2,1)} %values_hbm.1, ...), custom_call_target="tpu_custom_call" | custom-call | flops 10000000000 | bytes 10000000 | tf_op jit(solution)/shard_map/pallas_call | solution.py:315
  10.1 7.9 %collective-permute-done.weight_below = bf16[1024,256]{1,0:T(8,128)(2,1)S(1)} collective-permute-done((bf16[1024,256]{1,0:T(8,128)(2,1)}, bf16[1024,256]{1,0:T(8,128)(2,1)S(1)}, u32[]{:S(2)}, u32[]{:S(2)}) %collective-permute-start) | collective-permute-done | bytes 524320 | tf_op jit(solution)/shard_map/ppermute | solution.py:705
  18.0 0.0 collective-permute-done.1.weight_above
  18.0 0.0 copy-done
  18.0 58.8 %shard_map.92 = bf16[24,4,1024]{2,1,0:T(4,128)(2,1)S(1)} custom-call(bf16[8,2,3,128,128]{4,3,2,1,0:T(8,128)(2,1)} %get-tuple-element.7.part_hbm, f32[8,1024,128]{2,1,0:T(8,128)} %get-tuple-element.8.lse_hbm, bf16[1024,256]{1,0:T(8,128)(2,1)S(1)} %copy-done, bf16[1024,256]{1,0:T(8,128)(2,1)S(1)} %collective-permute-done.weight_below, ...), custom_call_target="tpu_custom_call" | custom-call | tf_op jit(solution)/shard_map/pallas_call | solution.py:662
  76.8 0.7 copy.11
Async XLA Ops:
  0.0 18.0 %collective-permute-start = (bf16[1024,256]{1,0:T(8,128)(2,1)}, bf16[1024,256]{1,0:T(8,128)(2,1)S(1)}, u32[]{:S(2)}, u32[]{:S(2)}) collective-permute-start(bf16[1024,256]{1,0:T(8,128)(2,1)} %weight_hbm.1), channel_id=1, source_target_pairs={{0,4},{1,5},{2,6},{3,7},{4,8},{5,9},{6,10},{7,11},{8,12},{9,13},{1... | collective-permute-start | bytes 1572872 | tf_op jit(solution)/shard_map/ppermute | solution.py:705
  1.9 16.1 %collective-permute-start.1 = (bf16[1024,256]{1,0:T(8,128)(2,1)}, bf16[1024,256]{1,0:T(8,128)(2,1)S(1)}, u32[]{:S(2)}, u32[]{:S(2)}) collective-permute-start(bf16[1024,256]{1,0:T(8,128)(2,1)} %weight_hbm.1), channel_id=1, source_target_pairs={{0,28},{1,29},{2,30},{3,31},{4,0},{5,1},{6,2},{7,3},{8,4},{9,5},{1... | collective-permute-start | bytes 1572872 | tf_op jit(solution)/shard_map/ppermute | solution.py:705
  5.9 12.1 %copy-start = (bf16[1024,256]{1,0:T(8,128)(2,1)S(1)}, bf16[1024,256]{1,0:T(8,128)(2,1)}, u32[]{:S(2)}) copy-start(bf16[1024,256]{1,0:T(8,128)(2,1)} %weight_hbm.1) | copy-start | bytes 1572868
